TPU v7x, 128 devices: a whole 4x4x4 slice. The times are simulated.
128 devices in a mesh: clus: 16 (over z, y_hi, core), dir: 8 (over x, y_lo).
Axes of the slice: x: 4, y: 4 (y_hi: 2, y_lo: 2; y = y_hi * 2 + y_lo), z: 4, core: 2. Of those that a mesh axis runs over, the one named last changes fastest.
Arguments:
- currents: bfloat16 [2, 512, 64, 128], P(None, 'clus', 'dir'), may hold values from -6 to 6
- cluster_size: int32 [512], P('clus'), may hold values from 32 to 128
- radiation: bfloat16 [2, 512, 256, 128], P(None, 'clus', 'dir'), may hold values from -0.5 to 0.5
- receive: bfloat16 [2, 512, 256, 128], P(None, 'clus', 'dir'), may hold values from -0.375 to 0.375
- phase: float32 [512, 512], P('clus', 'dir'), may hold values from -3.140625 to 3.140625
- interp: float32 [8, 64, 32], P('dir'), may hold values from -1 to 1
- trans: bfloat16 [2, 256, 64, 512], P(None, 'clus', None, 'dir'), may hold values from -0.75 to 0.75
- far_ids: int32 [256, 64], P('clus'), may hold values from 0 to 255
- far_live: int32 [256, 64], P('clus'), may hold values 0 or 1
- near_blocks: bfloat16 [2, 512, 16, 128, 128], P(None, 'clus', 'dir'), may hold values from -0.125 to 0.125
- near_offset: int32 [512, 16], P('clus', 'dir'), may hold values from -32 to 32
- near_live: int32 [512, 16], P('clus', 'dir'), may hold values 0 or 1
Outputs:
- field: bfloat16 [2, 512, 64, 128], P(None, 'clus', 'dir')
All inputs are finite; a program needn't handle non-finite values. No bound on the sum of `far_live` or of `near_live` on one device may be relied on, other than what follows from the above.
Results may differ from a plain program's by a relative error of at most 0.022.
Values may be sent and summed in bfloat16 or wider, within the bound.
No kernel may reach another device: no remote copies, remote signals or barrier semaphores. Data moves between devices by JAX's collectives and lax.ppermute only.
A program may use at most 128 MiB of HBM per device.

v0:
```python
import jax
import jax.numpy as jnp
from jax import lax
from jax.sharding import PartitionSpec as P


def with_halo(cells, sides, width):
    for axis, dim in sides:
        count = lax.axis_size(axis)
        ends = count - 1
        head = lax.slice_in_dim(cells, 0, width, axis=dim)
        tail = lax.slice_in_dim(cells, cells.shape[dim] - width, cells.shape[dim], axis=dim)
        cells = jnp.concatenate(
            [
                lax.ppermute(tail, axis, [(i, (i + 1) % count) for i in range(ends)]),
                cells,
                lax.ppermute(head, axis, [((i + 1) % count, i) for i in range(ends)]),
            ],
            axis=dim,
        )
    return cells


def complex_einsum(formula, former, latter):

    def single(first_part, second_part):
        return jnp.einsum(formula, first_part, second_part, preferred_element_type=jnp.float32)

    real_part = single(former[0], latter[0]) - single(former[1], latter[1])
    imag_part = single(former[0], latter[1]) + single(former[1], latter[0])
    return jnp.stack([real_part, imag_part])


def translate(sources, target_ids, factors):
    source_count = sources.shape[1]
    columns = jnp.arange(source_count, dtype=jnp.int32)
    selector = (target_ids[:, :, None] == columns[None, None, :]).astype(jnp.bfloat16)
    weights = jnp.einsum("rpjq,pjs->rqps", factors, selector, preferred_element_type=jnp.float32)
    leading = weights.astype(jnp.bfloat16)
    remainder = (weights - leading.astype(jnp.float32)).astype(jnp.bfloat16)
    total = complex_einsum("qps,sqe->pqe", leading, sources) + complex_einsum(
        "qps,sqe->pqe", remainder, sources
    )
    return total.astype(jnp.bfloat16)


def local(
    currents,
    cluster_size,
    radiation,
    receive,
    phase,
    interp,
    trans,
    far_ids,
    far_live,
    near_blocks,
    near_offset,
    near_live,
):
    highest = lax.Precision.HIGHEST
    clus_dev = currents.shape[1]
    unknowns = currents.shape[3]
    excite = currents.shape[2] * lax.axis_size("dir")
    clus_count = lax.axis_size("clus")
    clus_pos = lax.axis_index("clus")
    alive_mask = jnp.arange(unknowns, dtype=jnp.int32)[None, :] < cluster_size[:, None]
    masked = jnp.where(alive_mask[None, :, None, :], currents, jnp.zeros((), currents.dtype))
    complete = lax.all_gather(masked, "dir", axis=2, tiled=True)
    extended = with_halo(complete, (("clus", 1),), clus_dev)
    own_currents = extended[:, clus_dev : 2 * clus_dev]
    spectra = complex_einsum("ckm,cem->cke", radiation, own_currents)
    groups = interp.shape[0]
    group_len = interp.shape[2]
    leaf_dirs = spectra.shape[2]
    parent_dirs = 2 * leaf_dirs
    grouped = spectra.reshape(2, clus_dev, groups, group_len, excite)
    raised = jnp.einsum("ghk,rcgke->rcghe", interp, grouped, precision=highest).reshape(
        2, clus_dev, parent_dirs, excite
    )
    cosine = jnp.cos(phase)[:, :, None]
    sine = jnp.sin(phase)[:, :, None]
    shifted = jnp.stack(
        [cosine * raised[0] - sine * raised[1], sine * raised[0] + cosine * raised[1]]
    )
    parents = jnp.sum(shifted.reshape(2, clus_dev // 2, 2, parent_dirs, excite), axis=2).astype(
        jnp.bfloat16
    )
    factors = jnp.where(far_live[None, :, :, None] == 1, trans, jnp.zeros((), trans.dtype))
    gathered = lax.all_gather(parents, "clus", axis=1, tiled=True)
    translated = translate(gathered, far_ids, factors)
    twice = jnp.repeat(translated.astype(jnp.float32), 2, axis=1)
    downward = jnp.stack([cosine * twice[0] + sine * twice[1], cosine * twice[1] - sine * twice[0]])
    lowered = jnp.einsum(
        "ghk,rcghe->rcgke",
        interp,
        downward.reshape(2, clus_dev, groups, 2 * group_len, excite),
        precision=highest,
    )
    lowered = lowered.reshape(2, clus_dev, leaf_dirs, excite).astype(jnp.bfloat16)
    far_part = complex_einsum("cke,ckm->cem", lowered, receive)
    first_cluster = clus_pos * clus_dev
    cluster_rows = jnp.arange(clus_dev, dtype=jnp.int32)[:, None] + first_cluster
    source_ids = jnp.clip(cluster_rows + near_offset, 0, clus_dev * clus_count - 1) - (
        first_cluster - clus_dev
    )
    picked = jnp.take(extended, source_ids, axis=1)
    picked = jnp.where(near_live[None, :, :, None, None] == 1, picked, jnp.zeros((), picked.dtype))
    near_part = complex_einsum("cjmn,cjen->cem", near_blocks, picked)
    partial_sum = far_part + near_part
    summed = lax.psum_scatter(
        partial_sum.astype(jnp.bfloat16), "dir", scatter_dimension=2, tiled=True
    ).astype(jnp.float32)
    return jnp.where(alive_mask[None, :, None, :], summed, jnp.zeros((), summed.dtype)).astype(
        jnp.bfloat16
    )


def solution(mesh):
    in_specs = (
        P(None, "clus", "dir", None),
        P("clus"),
        P(None, "clus", "dir", None),
        P(None, "clus", "dir", None),
        P("clus", "dir"),
        P("dir", None, None),
        P(None, "clus", None, "dir"),
        P("clus", None),
        P("clus", None),
        P(None, "clus", "dir", None, None),
        P("clus", "dir"),
        P("clus", "dir"),
    )
    out_specs = P(None, "clus", "dir", None)
    return jax.shard_map(local, mesh=mesh, in_specs=in_specs, out_specs=out_specs, check_vma=False)
```

profile of v0, /device:TPU:0, one launch (start us, length us, event | category | flops | bytes accessed | tf_op | source)
XLA Modules:
  0.0 227.5 jit_solution(18075640560991071744)
XLA Ops:
  6.5 0.8 iota_compare_fusion.1
  7.3 1.6 broadcast_select_fusion.1
  9.0 0.8 fusion.140
  9.8 42.8 %all-gather.3.cloned.1.call-done = bf16[2,32,64,128]{3,2,1,0:T(8,128)(2,1)} async-done(((bf16[2,32,8,128]{3,2,1,0:T(8,128)(2,1)}), bf16[2,32,64,128]{3,2,1,0:T(8,128)(2,1)}) %all-gather.3.cloned.1.call-update) | async-done | bytes 1048592 | tf_op jit(solution)/shard_map/all_gather | solution.py:69
  52.6 1.6 fusion.106
  54.2 1.5 fusion.107
  55.7 0.4 fusion.93
  56.1 0.4 fusion.92
  56.4 3.5 %convolution_bitcast_fusion = f32[2,32,1,64,64]{3,4,1,0,2:T(8,128)S(1)} fusion(f32[1,32,32,64]{3,2,1,0:T(8,128)S(1)} %fusion.92, f32[1,32,32,64]{3,2,1,0:T(8,128)S(1)} %fusion.93, f32[1,64,32]{1,2,0:T(8,128)S(1)} %copy-done), kind=kOutput, calls=%fused_computation.43 | convolution fusion | flops 100794368 | bytes 1581056 | tf_op jit(solution)/shard_map/ghk,rcgke->rcghe/dot_general | solution.py:78
  60.2 0.5 multiply_subtract_fusion
  61.0 1.0 copy.43
  62.4 2.3 %collective-permute-start = (bf16[2,32,64,128]{3,2,1,0:T(8,128)(2,1)S(1)}, bf16[2,32,64,128]{3,2,1,0:T(8,128)(2,1)}, u32[]{:S(2)}, u32[]{:S(2)}) collective-permute-start(bf16[2,32,64,128]{3,2,1,0:T(8,128)(2,1)S(1)} %copy-done.3), channel_id=1, source_target_pairs={{0,8},{8,16},{16,24},{24,32},{32,40},{40,48},{48,56},{56,64},{64,7... | collective-permute-start | bytes 3145736 | tf_op jit(solution)/shard_map/ppermute | solution.py:15
  64.7 1.5 collective-permute-start.1
  66.3 1.1 fusion.21
  67.5 1.2 slice_bitcast_fusion.8
  68.7 4.2 %collective-permute-done.1 = bf16[2,32,64,128]{3,2,1,0:T(8,128)(2,1)} collective-permute-done((bf16[2,32,64,128]{3,2,1,0:T(8,128)(2,1)S(1)}, bf16[2,32,64,128]{3,2,1,0:T(8,128)(2,1)}, u32[]{:S(2)}, u32[]{:S(2)}) %collective-permute-start.1) | collective-permute-done | bytes 1048608 | tf_op jit(solution)/shard_map/ppermute | solution.py:17
  72.9 3.0 %pad_maximum_fusion = bf16[2,96,64,128]{3,2,1,0:T(8,128)(2,1)} fusion(bf16[2,32,64,128]{3,2,1,0:T(8,128)(2,1)} %collective-permute-done.1, bf16[2,32,64,128]{3,2,1,0:T(8,128)(2,1)S(1)} %copy-done.3, bf16[2,32,64,128]{3,2,1,0:T(8,128)(2,1)} %collective-permute-done), kind=kLoop, calls=%fused_computation.1 | loop fusion | flops 3145728 | bytes 6291456 | tf_op jit(solution)/shard_map/concatenate | solution.py:13
  75.9 3.0 %gather_fusion = bf16[64,2,64,128]{3,2,1,0:T(8,128)(2,1)S(1)} fusion(bf16[2,96,64,128]{3,2,1,0:T(8,128)(2,1)} %pad_maximum_fusion, s32[1024]{0:T(1024)S(1)} %pad_clamp_fusion), kind=kCustom, calls=%fused_computation | custom fusion | bytes 4194560 | tf_op jit(solution)/shard_map/jit(_take)/gather | solution.py:107
  79.3 1.8 copy-done.2
  81.1 0.8 fusion.39
  82.0 0.8 fusion.36
  82.8 1.8 fusion.53
  84.7 1.8 fusion.59
  86.5 62.1 %all-gather.5.cloned.1.call-done = bf16[2,256,64,64]{3,2,0,1:T(8,128)(2,1)} async-done(((bf16[2,16,64,64]{3,2,0,1:T(8,128)(2,1)}), bf16[2,256,64,64]{3,2,0,1:T(8,128)(2,1)}) %all-gather.5.cloned.1.call-update) | async-done | bytes 4194320 | tf_op jit(solution)/shard_map/all_gather | solution.py:90
  148.6 6.5 %fusion.138 = (bf16[1,256,64,64]{3,2,0,1:T(8,128)(2,1)}, bf16[1,256,64,64]{3,2,0,1:T(8,128)(2,1)}) fusion(bf16[2,256,64,64]{3,2,0,1:T(8,128)(2,1)} %all-gather.5.cloned.1.call-done), kind=kLoop, calls=%fused_computation.144 | loop fusion | bytes 8388608 | tf_op jit(solution)/shard_map/slice | solution.py:29
  155.1 5.9 %copy.72 = bf16[1,256,64,64]{1,3,2,0:T(8,128)(2,1)} copy(bf16[1,256,64,64]{3,2,0,1:T(8,128)(2,1)} %get-tuple-element.10) | data formatting | bytes 4194304
  161.0 4.9 %copy.71 = bf16[1,256,64,64]{1,3,2,0:T(8,128)(2,1)S(1)} copy(bf16[1,256,64,64]{3,2,0,1:T(8,128)(2,1)} %get-tuple-element.9) | data formatting | bytes 4194304
  165.9 2.5 %fusion.19 = f32[64,64,16]{1,2,0:T(8,128)S(1)} fusion(bf16[1,256,64,64]{1,3,2,0:T(8,128)(2,1)} %copy.72, bf16[64,16,256]{2,0,1:T(8,128)(2,1)} %get-tuple-element.26), kind=kOutput, calls=%fused_computation.23 | convolution fusion | flops 33554432 | bytes 2883584 | tf_op jit(solution)/shard_map/qps,sqe->pqe/dot_general | solution.py:27
  168.4 0.7 fusion.17
  169.1 0.7 fusion.71
  169.8 0.3 copy-done.4
  170.1 0.7 fusion.77
  170.8 0.7 fusion.15
  171.5 0.7 fusion.13
  172.2 0.7 fusion.83
  172.9 0.7 fusion.89
  174.4 0.9 fusion.94
  175.4 1.4 fusion.65
  176.8 0.3 fusion.120
  177.5 0.3 fusion.49
  177.8 0.3 fusion.48
  178.2 0.5 copy-done.6
  179.0 0.5 fusion.4
  179.5 0.7 copy.69
  180.2 1.7 copy.102
  181.9 37.3 %reduce-scatter.4.cloned.1.call-done = bf16[8,8192]{1,0:T(8,128)(2,1)} async-done(((bf16[64,8192]{1,0:T(8,128)(2,1)}), bf16[8,8192]{1,0:T(8,128)(2,1)}) %reduce-scatter.4.cloned.1.call-update) | async-done | bytes 131088
  219.2 0.9 copy.74
  220.2 0.8 select_convert_fusion
  (53 shorter events, 2.9 us)
Async XLA Ops:
  6.5 49.9 %copy-start = (f32[1,64,32]{1,2,0:T(8,128)S(1)}, f32[1,64,32]{1,2,0:T(8,128)}, u32[]{:S(2)}) copy-start(f32[1,64,32]{1,2,0:T(8,128)} %param.17) | copy-start | bytes 24580
  6.5 49.1 %copy-start.8 = (bf16[2,32,32,128]{3,2,1,0:T(8,128)(2,1)S(1)}, bf16[2,32,32,128]{3,2,1,0:T(8,128)(2,1)}, u32[]{:S(2)}) copy-start(bf16[2,32,32,128]{3,2,1,0:T(8,128)(2,1)} %param.14) | copy-start | bytes 1572868
  6.5 46.0 %all-gather.3.cloned.1.call-start = ((), (), s32[]{:S(2)}) async-start(), calls=%async_computation.1 | async-start | bytes 1179648 | tf_op jit(solution)/shard_map/all_gather | solution.py:69
  8.9 139.7 %all-gather.5.cloned.1.call-start = ((), (), s32[]{:S(2)}) async-start(), calls=%async_computation.2 | async-start | bytes 8912896 | tf_op jit(solution)/shard_map/all_gather | solution.py:90
  52.6 3.1 %copy-start.3 = (bf16[2,32,64,128]{3,2,1,0:T(8,128)(2,1)S(1)}, bf16[2,32,64,128]{3,2,1,0:T(8,128)(2,1)}, u32[]{:S(2)}) copy-start(bf16[2,32,64,128]{3,2,1,0:T(8,128)(2,1)} %all-gather.3.cloned.1.call-done) | copy-start | bytes 3145732
  60.7 1.4 copy-start.13
  60.7 5.5 %copy-start.14 = (s32[32,2]{0,1:T(2,128)S(1)}, s32[32,2]{0,1:T(2,128)}, u32[]{:S(2)}) copy-start(s32[32,2]{0,1:T(2,128)} %param.23) | copy-start | bytes 772
  60.7 5.6 %copy-start.12 = (s32[16,64]{1,0:T(8,128)S(1)}, s32[16,64]{1,0:T(8,128)}, u32[]{:S(2)}) copy-start(s32[16,64]{1,0:T(8,128)} %param.20) | copy-start | bytes 12292
  60.7 5.6 %copy-start.10 = (bf16[2,16,64,64]{3,2,1,0:T(8,128)(2,1)S(1)}, bf16[2,16,64,64]{3,2,1,0:T(8,128)(2,1)}, u32[]{:S(2)}) copy-start(bf16[2,16,64,64]{3,2,1,0:T(8,128)(2,1)} %param.18) | copy-start | bytes 786436
  60.7 5.6 %copy-start.11 = (s32[16,64]{1,0:T(8,128)S(1)}, s32[16,64]{1,0:T(8,128)}, u32[]{:S(2)}) copy-start(s32[16,64]{1,0:T(8,128)} %param.19) | copy-start | bytes 12292
  62.0 157.2 %reduce-scatter.4.cloned.1.call-start = ((), (), s32[]{:S(2)}) async-start(), calls=%async_computation.3 | async-start | bytes 1179648
  62.4 6.3 %collective-permute-start = (bf16[2,32,64,128]{3,2,1,0:T(8,128)(2,1)S(1)}, bf16[2,32,64,128]{3,2,1,0:T(8,128)(2,1)}, u32[]{:S(2)}, u32[]{:S(2)}) collective-permute-start(bf16[2,32,64,128]{3,2,1,0:T(8,128)(2,1)S(1)} %copy-done.3), channel_id=1, source_target_pairs={{0,8},{8,16},{16,24},{24,32},{32,40},{40,48},{48,56},{56,64},{64,7... | collective-permute-start | bytes 3145736 | tf_op jit(solution)/shard_map/ppermute | solution.py:15
  64.7 8.2 %collective-permute-start.1 = (bf16[2,32,64,128]{3,2,1,0:T(8,128)(2,1)S(1)}, bf16[2,32,64,128]{3,2,1,0:T(8,128)(2,1)}, u32[]{:S(2)}, u32[]{:S(2)}) collective-permute-start(bf16[2,32,64,128]{3,2,1,0:T(8,128)(2,1)S(1)} %copy-done.3), channel_id=1, source_target_pairs={{8,0},{16,8},{24,16},{32,24},{40,32},{48,40},{56,48},{64,56},{72,6... | collective-permute-start | bytes 3145736 | tf_op jit(solution)/shard_map/ppermute | solution.py:17
  78.9 2.2 copy-start.2
  165.9 2.5 %copy-start.1 = (bf16[1,256,64,64]{1,3,2,0:T(8,128)(2,1)S(1)}, bf16[1,256,64,64]{1,3,2,0:T(8,128)(2,1)}, u32[]{:S(2)}) copy-start(bf16[1,256,64,64]{1,3,2,0:T(8,128)(2,1)} %copy.72) | copy-start | bytes 6291460
  165.9 2.5 %copy-start.5 = (bf16[64,16,256]{2,0,1:T(8,128)(2,1)S(1)}, bf16[64,16,256]{2,0,1:T(8,128)(2,1)}, u32[]{:S(2)}) copy-start(bf16[64,16,256]{2,0,1:T(8,128)(2,1)} %get-tuple-element.25) | copy-start | bytes 1572868
  169.1 1.0 copy-start.4
  175.4 1.4 copy-start.9
  177.5 1.2 copy-start.6
  177.5 1.5 copy-start.7
Sparse Core Ops, SparseCore 0:
  9.1 43.4 all-gather.2
  62.1 86.4 all-gather.4
  182.0 37.1 reduce-scatter.3
where the time goes:
time: 228 us; the launch traced here: 227 us
  waiting for transfers between devices  147 us (64%)
  local copies, waits for them, and re-layouts  31 us (14%)
  matrix products  23.9 us (10%)
  between operations  13.5 us (6%)
  other arithmetic  8.76 us (4%)
  starting transfers between devices  3.85 us (2%)
    all_gather x1, waiting for transfers between devices, local(): gathered = lax.all_gather(parents, 'clus', axis=1, tiled=True)  62.1 us
    all_gather x1, waiting for transfers between devices, local(): complete = lax.all_gather(masked, 'dir', axis=2, tiled=True)  42.8 us
    unnamed x4, waiting for transfers between devices  37.4 us
    dot_general x20, matrix products, single(): jnp.einsum(formula, first_part, second_part, preferred_element_type=jnp.f...  17.8 us
    unnamed x35, local copies, waits for them, and re-layouts  17.2 us
    slice x1, local copies, waits for them, and re-layouts, complex_einsum(): real_part = single(former[0], latter[0]) - single(former[1], latter[1])  6.49 us
  transfers between devices with their start and end apart: 5, of which 4 were waited for; matrix products, arithmetic and copies ran while one was open for 7% of the time, Pallas kernels for 0%

commit v1 on v0

v1 whole, which is shorter than its diff:
```python
import jax
import jax.numpy as jnp
from jax import lax
from jax.experimental import pallas as pl
from jax.experimental.pallas import tpu as pltpu
from jax.sharding import PartitionSpec as P

BF = jnp.bfloat16
F32 = jnp.float32
NT = (((1,), (1,)), ((), ()))
NN = (((1,), (0,)), ((), ()))
TN = (((0,), (0,)), ((), ()))
VMEM = pl.BlockSpec(memory_space=pltpu.VMEM)
SMEM = pl.BlockSpec(memory_space=pltpu.SMEM)


def dot(a, b, dims):
    return lax.dot_general(a, b, dims, preferred_element_type=F32)


def params(mib):
    return pltpu.CompilerParams(vmem_limit_bytes=mib * 2**20)


def turn_lanes(x):
    lane = lax.broadcasted_iota(jnp.int32, x.shape, 1)
    return jnp.where(lane % 16 < 8, -pltpu.roll(x, 120, 1), pltpu.roll(x, 8, 1))


def turn_rows(x):
    y = x.reshape(8, 2, 8, x.shape[1])
    return jnp.stack([-y[:, 1], y[:, 0]], axis=1).reshape(x.shape)


def pack_kernel(trans, live, ids, out, rows):
    for pp in range(8):
        for r in range(2):
            tiles = []
            for p in (2 * pp, 2 * pp + 1):
                tile = trans[r, p].astype(F32).T
                tiles.append(jnp.where(live[pl.ds(p, 1), :] == 1, tile, 0.0))
            rows[pl.ds(r * 8 + pp, 64, stride=16), :] = jnp.concatenate(tiles, axis=1)
    out[:, 0:64, :] = rows[...].reshape(16, 64, 128).astype(BF)
    pairs = ids[...].astype(F32)
    pairs = jnp.concatenate([pairs, jnp.zeros((8, 128), F32)], axis=0).astype(BF)
    out[:, 64:80, :] = jnp.broadcast_to(pairs[None], (16, 16, 128))


def weights_kernel(packed, out, rows, ids, sums):
    rows[...] = packed[:, 0:64, :].astype(F32).reshape(1024, 128)
    ids[...] = packed[:, 64:80, :].astype(F32)[:, 0:8, :].reshape(128, 128).astype(jnp.int32)
    lane = lax.broadcasted_iota(jnp.int32, (8, 128), 1)
    source = lax.broadcasted_iota(jnp.int32, (256, 128), 0)

    def step(i, carry):
        factors = rows[pl.ds((i // 8) * 64 + i % 8, 8, stride=8), :]
        left = jnp.concatenate(
            [jnp.where(lane < 64, factors, 0.0), jnp.where(lane < 64, 0.0, factors)], axis=0
        ).astype(BF)
        hit = jnp.where(source == ids[pl.ds(i, 1), :], 1.0, 0.0).astype(BF)
        made = dot(left, hit, NT)
        for b in range(2):
            for h in range(2):
                sums[h, pl.ds(2 * i + b, 8, stride=256), :] = made[
                    b * 8 : b * 8 + 8, h * 128 : h * 128 + 128
                ]
        return carry

    lax.fori_loop(0, 128, step, 0, unroll=8)
    out[...] = sums[...].astype(BF)


def fold_kernel(radiation, receive, phase, interp4, up, down):
    cosine = jnp.cos(phase[...])
    sine = jnp.sin(phase[...])
    raise4 = interp4[...].astype(BF)
    for g in range(8):
        sent = [dot(raise4, radiation[r, g * 4 : g * 4 + 4].reshape(128, 128), NN) for r in range(2)]
        got = [dot(raise4, receive[r, g * 4 : g * 4 + 4].reshape(128, 128), NN) for r in range(2)]
        for n in range(4):
            c = g * 4 + n
            co = jnp.broadcast_to(cosine[:, c : c + 1], (64, 128))
            si = jnp.broadcast_to(sine[:, c : c + 1], (64, 128))
            ur, ui = (s[n * 64 : n * 64 + 64] for s in sent)
            vr, vi = (s[n * 64 : n * 64 + 64] for s in got)
            b = (c % 2) * 128
            up[c // 2, 0:64, b : b + 128] = (co * ur - si * ui).astype(BF)
            up[c // 2, 64:128, b : b + 128] = (si * ur + co * ui).astype(BF)
            down[c, :, 0:128] = (co * vr + si * vi).astype(BF)
            down[c, :, 128:256] = (co * vi - si * vr).astype(BF)


def parents_kernel(everyone, up, out, rows):
    for p in range(16):
        x = jnp.concatenate(
            [everyone[:, 2 * p + b].reshape(128, 128) for b in range(2)], axis=1
        )
        y = dot(up[p], x, NT)
        rows[pl.ds(p, 64, stride=16), :] = y[0:64] + turn_lanes(y[64:128])
    out[...] = rows[...].reshape(16, 64, 128).astype(BF)


def translate_kernel(sources, weights, out):
    for q in range(4):
        src = sources[:, q * 16 : q * 16 + 16, :].reshape(256, 128)
        w = slice(q * 512, q * 512 + 512)
        z = dot(weights[0, w, :], src[0:128], NN) + dot(weights[1, w, :], src[128:256], NN)
        done = z[0:256] + turn_lanes(z[256:512])
        out[:, q * 16 : q * 16 + 16, :] = done.reshape(16, 16, 128).astype(BF)


def near_kernel(place, offset, live, own, partner, far, blocks, out, cells):
    first = place[0] * 32
    even = place[0] % 2 == 0
    cells[:, 32:64] = own[...]
    cells[:, pl.ds(jnp.where(even, 64, 0), 32)] = partner[...]
    cells[:, pl.ds(jnp.where(even, 0, 64), 32)] = far[...]
    last = place[1] * 32 - 1

    def step(c, carry):
        total = [jnp.zeros((128, 128), F32), jnp.zeros((128, 128), F32)]
        for j in range(2):
            source = jnp.clip(first + c + offset[c, j], 0, last) - first + 32
            x = cells[:, source].reshape(128, 128)
            x = jnp.where(live[c, j] == 1, x, jnp.zeros_like(x))
            for r in range(2):
                total[r] += dot(x, blocks[r, c, j], NT)
        out[c] = (total[0] + turn_rows(total[1])).astype(BF)
        return carry

    lax.fori_loop(0, 32, step, 0, unroll=4)


def far_kernel(translated, down, near, out, rows):
    rows[...] = translated[...].astype(F32).reshape(1024, 128)
    for p in range(16):
        t = rows[pl.ds(p, 64, stride=16), :].T.astype(BF)
        for c in (2 * p, 2 * p + 1):
            y = dot(t, down[c], NN)
            field = y[:, 0:128] + turn_rows(y[:, 128:256]) + near[c].astype(F32)
            out[:, c] = field.reshape(8, 16, 128).astype(BF)


def call(kernel, shape, scratch, mib, specs, cost, dtype=BF):
    many = isinstance(shape, list)
    outs = [jax.ShapeDtypeStruct(s, dtype) for s in (shape if many else [shape])]
    return pl.pallas_call(
        kernel,
        out_shape=outs if many else outs[0],
        in_specs=specs,
        out_specs=[VMEM] * len(outs) if many else VMEM,
        scratch_shapes=scratch,
        compiler_params=params(mib),
        cost_estimate=pl.CostEstimate(flops=cost[0], bytes_accessed=cost[1], transcendentals=0),
    )


def local(
    currents,
    cluster_size,
    radiation,
    receive,
    phase,
    interp,
    trans,
    far_ids,
    far_live,
    near_blocks,
    near_offset,
    near_live,
):
    place = lax.axis_index("clus")
    count = lax.axis_size("clus")
    alive = lax.broadcasted_iota(jnp.int32, (32, 128), 1) < cluster_size[:, None]

    packed = call(
        pack_kernel, (16, 80, 128), [pltpu.VMEM((1024, 128), F32)], 16, [VMEM] * 3, (1, 2**20)
    )(trans, far_live, far_ids.reshape(8, 128))
    packed = lax.all_to_all(packed, "clus", 0, 0)

    masked = jnp.where(alive[None, :, None, :], currents, jnp.zeros((), BF))
    masked = masked.transpose(1, 0, 2, 3).reshape(1, 32, 16, 128)
    everyone = lax.all_to_all(jnp.broadcast_to(masked, (8, 32, 16, 128)), "dir", 0, 0)

    weights = call(
        weights_kernel,
        (2, 2048, 128),
        [
            pltpu.VMEM((1024, 128), F32),
            pltpu.VMEM((128, 128), jnp.int32),
            pltpu.VMEM((2, 2048, 128), F32),
        ],
        24,
        [VMEM],
        (2**32, 2**23),
    )(packed)
    interp4 = jnp.kron(jnp.eye(4, dtype=F32), interp[0])
    up, down = call(
        fold_kernel, [(16, 128, 256), (32, 64, 256)], [], 24, [VMEM] * 4, (2**31, 2**23)
    )(radiation, receive, phase.T, interp4)

    rows = pltpu.VMEM((1024, 128), F32)
    parents = call(parents_kernel, (16, 64, 128), [rows], 24, [VMEM] * 2, (2**27, 2**21))(
        everyone, up
    )
    partner = lax.ppermute(everyone, "clus", [(i, i ^ 1) for i in range(count)])
    across = [(i, i + 1) for i in range(1, count - 1, 2)]
    far = lax.ppermute(everyone, "clus", across + [(b, a) for a, b in across])
    sources = lax.all_to_all(parents, "clus", 0, 0)
    translated = call(translate_kernel, (16, 64, 128), [], 24, [VMEM] * 2, (2**28, 2**21))(
        sources, weights
    )
    back = lax.all_to_all(translated, "clus", 0, 0)
    near = call(
        near_kernel,
        (32, 128, 128),
        [pltpu.VMEM((8, 96, 16, 128), BF)],
        32,
        [SMEM] * 3 + [VMEM] * 4,
        (2**32, 2**23),
    )(jnp.stack([place, count]).astype(jnp.int32), near_offset, near_live, everyone, partner, far, near_blocks)
    partial = call(far_kernel, (8, 32, 16, 128), [rows], 24, [VMEM] * 3, (2**28, 2**22))(
        back, down, near
    )
    shares = lax.all_to_all(partial, "dir", 0, 0)
    field = jnp.sum(shares.astype(F32), axis=0).reshape(32, 2, 8, 128)
    field = jnp.where(alive[:, None, None, :], field, 0.0).astype(BF)
    return field.transpose(1, 0, 2, 3)


def solution(mesh):
    in_specs = (
        P(None, "clus", "dir", None),
        P("clus"),
        P(None, "clus", "dir", None),
        P(None, "clus", "dir", None),
        P("clus", "dir"),
        P("dir", None, None),
        P(None, "clus", None, "dir"),
        P("clus", None),
        P("clus", None),
        P(None, "clus", "dir", None, None),
        P("clus", "dir"),
        P("clus", "dir"),
    )
    out_specs = P(None, "clus", "dir", None)
    return jax.shard_map(local, mesh=mesh, in_specs=in_specs, out_specs=out_specs, check_vma=False)
```

time: 228 us -> 102 us (0.45)
  waiting for transfers between devices: 147 us -> 26.9 us
  matrix products: 23.9 us -> 0 us
  starting transfers between devices: 3.85 us -> 26.3 us
  local copies, waits for them, and re-layouts: 31 us -> 12.4 us
  blocking collectives: 0 us -> 17.8 us
  Pallas kernels: 0 us -> 15.6 us
  between operations: 13.5 us -> 0.12 us
  other arithmetic: 8.76 us -> 2.07 us
    all_gather x2 -> x0, waiting for transfers between devices: 105 us -> none  [the longest x1 62.1 us: local(): gathered = lax.all_gather(parents, 'clus', axis=1, tiled=True)]
    unnamed x4 -> x0, waiting for transfers between devices: 37.4 us -> none
    all_to_all x0 -> x4, waiting for transfers between devices: none -> 26.9 us  [the longest x1 12 us: local(): lax.all_to_all(jnp.broadcast_to(masked, (8, 32, 16, 128)), 'dir', 0, 0)]
    all_to_all x0 -> x4, starting transfers between devices: none -> 24.3 us  [the longest x1 7.76 us: local(): packed = lax.all_to_all(packed, 'clus', 0, 0)]
    dot_general x23 -> x0, matrix products: 23.9 us -> none  [the longest x20 17.8 us: single(): jnp.einsum(formula, first_part, second_part, preferred_element_type=jnp.f...]
    all_to_all x0 -> x1, blocking collectives: none -> 17.8 us  [local(): shares = lax.all_to_all(partial, 'dir', 0, 0)]
    pallas_call x0 -> x7, Pallas kernels: none -> 15.6 us  [the longest x1 5.6 us: local(): call(near_kernel, (32, 128, 128), [pltpu.VMEM((8, 96, 16, 128), BF)], 32,...]
    unnamed x35 -> x27, local copies, waits for them, and re-layouts: 17.2 us -> 8.87 us
  transfers between devices with their start and end apart: 5 -> 6, of which waited for: 4 -> 4; matrix products, arithmetic and copies ran while one was open for 7% -> 2% of each run, Pallas kernels for 0% -> 15%
where the time goes in v1:
time: 102 us; the launch traced here: 101 us
  waiting for transfers between devices  26.9 us (26%)
  starting transfers between devices  26.3 us (26%)
  blocking collectives  17.8 us (17%)
  Pallas kernels  15.6 us (15%)
  local copies, waits for them, and re-layouts  12.4 us (12%)
  other arithmetic  2.07 us (2%)
    all_to_all x1, blocking collectives, local(): shares = lax.all_to_all(partial, 'dir', 0, 0)  17.8 us
    all_to_all x1, waiting for transfers between devices, local(): lax.all_to_all(jnp.broadcast_to(masked, (8, 32, 16, 128)), 'dir', 0, 0)  12 us
    all_to_all x1, waiting for transfers between devices, local(): sources = lax.all_to_all(parents, 'clus', 0, 0)  11.5 us
    unnamed x27, local copies, waits for them, and re-layouts  8.87 us
    all_to_all x1, starting transfers between devices, local(): packed = lax.all_to_all(packed, 'clus', 0, 0)  7.76 us
    all_to_all x1, starting transfers between devices, local(): sources = lax.all_to_all(parents, 'clus', 0, 0)  6.39 us
    pallas_call x1, Pallas kernels, local(): call(near_kernel, (32, 128, 128), [pltpu.VMEM((8, 96, 16, 128), BF)], 32,...  5.6 us
    all_to_all x1, starting transfers between devices, local(): lax.all_to_all(jnp.broadcast_to(masked, (8, 32, 16, 128)), 'dir', 0, 0)  5.41 us
  transfers between devices with their start and end apart: 6, of which 4 were waited for; matrix products, arithmetic and copies ran while one was open for 2% of the time, Pallas kernels for 15%

profile of v1, /device:TPU:0, one launch (start us, length us, event | category | flops | bytes accessed | tf_op | source)
XLA Modules:
  0.0 101.2 jit_solution(17137093371118283310)
XLA Ops:
  0.0 0.0 copy-start.10
  0.0 0.8 iota_compare_fusion
  0.8 0.9 fusion.2
  1.7 1.1 %broadcast_in_dim.42 = bf16[8,32,16,128]{3,2,1,0:T(8,128)(2,1)} broadcast(bf16[32,16,128]{2,1,0:T(8,128)(2,1)S(1)} %fusion.2), dimensions={1,2,3} | broadcast | bytes 1179648 | tf_op jit(solution)/shard_map/broadcast_in_dim | solution.py:183
  2.8 5.4 %all-to-all-start = ((bf16[8,32,16,128]{3,2,1,0:T(8,128)(2,1)}), bf16[8,32,16,128]{3,2,1,0:T(8,128)(2,1)S(1)}, u32[]{:S(2)}, u32[]{:S(2)}) async-start(bf16[8,32,16,128]{3,2,1,0:T(8,128)(2,1)} %broadcast_in_dim.42), calls=%async_computation | async-start | bytes 2097152 | tf_op jit(solution)/shard_map/all_to_all | solution.py:183
  8.3 0.8 reshape.51.ids
  9.0 1.0 %copy-done = bf16[2,16,64,64]{3,2,1,0:T(8,128)(2,1)S(1)} copy-done((bf16[2,16,64,64]{3,2,1,0:T(8,128)(2,1)S(1)}, bf16[2,16,64,64]{3,2,1,0:T(8,128)(2,1)}, u32[]{:S(2)}) %copy-start) | copy-done | bytes 262168
  10.1 0.7 copy-done.4
  10.8 1.2 %shard_map.120 = bf16[16,80,128]{2,1,0:T(8,128)(2,1)} custom-call(bf16[2,16,64,64]{3,2,1,0:T(8,128)(2,1)S(1)} %copy-done, s32[16,64]{1,0:T(8,128)S(1)} %copy-done.4, s32[8,128]{1,0:T(8,128)S(1)} %reshape.51.ids), custom_call_target="tpu_custom_call" | custom-call | flops 1 | bytes 1048576 | tf_op jit(solution)/shard_map/pallas_call | solution.py:176
  11.9 0.0 copy-done.10
  11.9 0.1 copy.20.offset
  12.0 0.0 copy-done.11
  12.0 0.1 copy.21.live
  12.1 12.0 %all-to-all-done.everyone.own = bf16[8,32,16,128]{3,2,1,0:T(8,128)(2,1)S(1)} async-done(((bf16[8,32,16,128]{3,2,1,0:T(8,128)(2,1)}), bf16[8,32,16,128]{3,2,1,0:T(8,128)(2,1)S(1)}, u32[]{:S(2)}, u32[]{:S(2)}) %all-to-all-start) | async-done | bytes 1048608 | tf_op jit(solution)/shard_map/all_to_all | solution.py:183
  24.1 7.8 %all-to-all-start.2 = ((bf16[16,80,128]{2,1,0:T(8,128)(2,1)}), bf16[16,80,128]{2,1,0:T(8,128)(2,1)S(1)}, u32[]{:S(2)}, u32[]{:S(2)}) async-start(bf16[16,80,128]{2,1,0:T(8,128)(2,1)} %shard_map.120), calls=%async_computation.2 | async-start | bytes 655360 | tf_op jit(solution)/shard_map/all_to_all | solution.py:179
  31.9 0.4 collective-permute-start
  32.3 1.6 %collective-permute-start.1 = (bf16[8,32,16,128]{3,2,1,0:T(8,128)(2,1)S(1)}, bf16[8,32,16,128]{3,2,1,0:T(8,128)(2,1)}, u32[]{:S(2)}, u32[]{:S(2)}) collective-permute-start(bf16[8,32,16,128]{3,2,1,0:T(8,128)(2,1)S(1)} %all-to-all-done.everyone.own), channel_id=1, source_target_pairs={{8,16},{24,32},{40,48},{56,64},{72,80},{88,96},{104,112},{16,8},{3... | collective-permute-start | bytes 3145736 | tf_op jit(solution)/shard_map/ppermute | solution.py:208
  33.9 0.0 copy-done.8
  33.9 0.1 broadcast_multiply_fusion
  34.0 0.2 mul.30
  34.2 0.8 copy.19.interp4
  35.0 0.0 copy-done.9
  35.0 0.1 copy.18
  35.1 0.1 pad_add_fusion.place
  35.2 0.9 copy-done.3
  36.1 1.0 %copy-done.6 = bf16[2,32,32,128]{3,2,1,0:T(8,128)(2,1)S(1)} copy-done((bf16[2,32,32,128]{3,2,1,0:T(8,128)(2,1)S(1)}, bf16[2,32,32,128]{3,2,1,0:T(8,128)(2,1)}, u32[]{:S(2)}) %copy-start.6) | copy-done | bytes 524312
  37.1 1.0 %copy-done.7 = bf16[2,32,32,128]{3,2,1,0:T(8,128)(2,1)S(1)} copy-done((bf16[2,32,32,128]{3,2,1,0:T(8,128)(2,1)S(1)}, bf16[2,32,32,128]{3,2,1,0:T(8,128)(2,1)}, u32[]{:S(2)}) %copy-start.7) | copy-done | bytes 524312
  38.1 1.0 shard_map.118
  39.1 1.3 %shard_map.119 = bf16[16,64,128]{2,1,0:T(8,128)(2,1)} custom-call(bf16[8,32,16,128]{3,2,1,0:T(8,128)(2,1)S(1)} %all-to-all-done.everyone.own, bf16[16,128,256]{2,1,0:T(8,128)(2,1)S(1)} %get-tuple-element.7.up), custom_call_target="tpu_custom_call" | custom-call | flops 134217728 | bytes 2097152 | tf_op jit(solution)/shard_map/pallas_call | solution.py:203
  40.4 1.7 %all-to-all-done.2.packed = bf16[16,80,128]{2,1,0:T(8,128)(2,1)S(1)} async-done(((bf16[16,80,128]{2,1,0:T(8,128)(2,1)}), bf16[16,80,128]{2,1,0:T(8,128)(2,1)S(1)}, u32[]{:S(2)}, u32[]{:S(2)}) %all-to-all-start.2) | async-done | bytes 327712 | tf_op jit(solution)/shard_map/all_to_all | solution.py:179
  42.1 0.7 copy-done.1
  42.8 6.4 %all-to-all-start.1 = ((bf16[16,64,128]{2,1,0:T(8,128)(2,1)}), bf16[16,64,128]{2,1,0:T(8,128)(2,1)S(1)}, u32[]{:S(2)}, u32[]{:S(2)}) async-start(bf16[16,64,128]{2,1,0:T(8,128)(2,1)} %shard_map.119), calls=%async_computation.1 | async-start | bytes 524288 | tf_op jit(solution)/shard_map/all_to_all | solution.py:209
  49.2 0.0 copy-start.2
  49.3 1.0 copy-done.2
  50.2 4.5 %shard_map.121.weights = bf16[2,2048,128]{2,1,0:T(8,128)(2,1)S(1)} custom-call(bf16[16,80,128]{2,1,0:T(8,128)(2,1)S(1)} %copy-done.2), custom_call_target="tpu_custom_call" | custom-call | flops 4294967296 | bytes 8388608 | tf_op jit(solution)/shard_map/pallas_call | solution.py:185
  54.7 11.5 %all-to-all-done.1.sources = bf16[16,64,128]{2,1,0:T(8,128)(2,1)S(1)} async-done(((bf16[16,64,128]{2,1,0:T(8,128)(2,1)}), bf16[16,64,128]{2,1,0:T(8,128)(2,1)S(1)}, u32[]{:S(2)}, u32[]{:S(2)}) %all-to-all-start.1) | async-done | bytes 262176 | tf_op jit(solution)/shard_map/all_to_all | solution.py:209
  66.2 1.3 %shard_map.122 = bf16[16,64,128]{2,1,0:T(8,128)(2,1)} custom-call(bf16[16,64,128]{2,1,0:T(8,128)(2,1)S(1)} %all-to-all-done.1.sources, bf16[2,2048,128]{2,1,0:T(8,128)(2,1)S(1)} %shard_map.121.weights), custom_call_target="tpu_custom_call" | custom-call | flops 268435456 | bytes 2097152 | tf_op jit(solution)/shard_map/pallas_call | solution.py:210
  67.5 4.7 %all-to-all-start.3 = ((bf16[16,64,128]{2,1,0:T(8,128)(2,1)}), bf16[16,64,128]{2,1,0:T(8,128)(2,1)S(1)}, u32[]{:S(2)}, u32[]{:S(2)}) async-start(bf16[16,64,128]{2,1,0:T(8,128)(2,1)} %shard_map.122), calls=%async_computation.3 | async-start | bytes 524288 | tf_op jit(solution)/shard_map/all_to_all | solution.py:213
  72.2 0.0 collective-permute-done.partner
  72.2 0.0 collective-permute-done.1.far
  72.2 0.0 copy-start.5
  72.2 2.2 %copy-done.5 = bf16[2,32,2,128,128]{4,3,2,1,0:T(8,128)(2,1)S(1)} copy-done((bf16[2,32,2,128,128]{4,3,2,1,0:T(8,128)(2,1)S(1)}, bf16[2,32,2,128,128]{4,3,2,1,0:T(8,128)(2,1)}, u32[]{:S(2)}) %copy-start.5) | copy-done | bytes 4194328
  74.4 5.6 %shard_map.123.near = bf16[32,128,128]{2,1,0:T(8,128)(2,1)S(1)} custom-call(s32[2]{0:T(128)S(1)} %pad_add_fusion.place, s32[32,2]{1,0:T(8,128)S(1)} %copy.20.offset, s32[32,2]{1,0:T(8,128)S(1)} %copy.21.live, bf16[8,32,16,128]{3,2,1,0:T(8,128)(2,1)S(1)} %all-to-all-done.everyone.own, bf16[8,32,16,128]{3,2,1,0:T(8,128)(2,1)} %collective-permute-done.partner, ...), custom_call_target="tpu_custom_call" | custom-call | flops 4294967296 | bytes 8388608 | tf_op jit(solution)/shard_map/pallas_call | solution.py:214
  80.0 1.7 %all-to-all-done.3.translated = bf16[16,64,128]{2,1,0:T(8,128)(2,1)S(1)} async-done(((bf16[16,64,128]{2,1,0:T(8,128)(2,1)}), bf16[16,64,128]{2,1,0:T(8,128)(2,1)S(1)}, u32[]{:S(2)}, u32[]{:S(2)}) %all-to-all-start.3) | async-done | bytes 262176 | tf_op jit(solution)/shard_map/all_to_all | solution.py:213
  81.7 0.8 shard_map.124
  82.5 17.8 %all_to_all.25 = bf16[8,32,16,128]{3,2,1,0:T(8,128)(2,1)S(1)} all-to-all(bf16[8,32,16,128]{3,2,1,0:T(8,128)(2,1)S(1)} %shard_map.124), channel_id=1, replica_groups=mesh['clus'=16,'dir'=8] {'dir'}, dimensions={0} | all-to-all | bytes 2097152 | tf_op jit(solution)/shard_map/all_to_all | solution.py:225
  100.3 0.1 convert_reduce_fusion
  100.5 0.7 copy.22
  (11 shorter events, 0.1 us)
Async XLA Ops:
  0.0 11.9 %copy-start.10 = (s32[32,2]{0,1:T(2,128)S(1)}, s32[32,2]{0,1:T(2,128)}, u32[]{:S(2)}) copy-start(s32[32,2]{0,1:T(2,128)} %param.22) | copy-start | bytes 772
  0.0 12.0 %copy-start.11 = (s32[32,2]{0,1:T(2,128)S(1)}, s32[32,2]{0,1:T(2,128)}, u32[]{:S(2)}) copy-start(s32[32,2]{0,1:T(2,128)} %param.23) | copy-start | bytes 772
  0.0 33.9 %copy-start.8 = (f32[1,64,32]{1,2,0:T(8,128)S(1)}, f32[1,64,32]{1,2,0:T(8,128)}, u32[]{:S(2)}) copy-start(f32[1,64,32]{1,2,0:T(8,128)} %param.17) | copy-start | bytes 24580
  0.0 35.0 %copy-start.9 = (f32[32,64]{1,0:T(8,128)S(1)}, f32[32,64]{1,0:T(8,128)}, u32[]{:S(2)}) copy-start(f32[32,64]{1,0:T(8,128)} %param.16) | copy-start | bytes 24580
  2.8 21.3 %all-to-all-start = ((bf16[8,32,16,128]{3,2,1,0:T(8,128)(2,1)}), bf16[8,32,16,128]{3,2,1,0:T(8,128)(2,1)S(1)}, u32[]{:S(2)}, u32[]{:S(2)}) async-start(bf16[8,32,16,128]{3,2,1,0:T(8,128)(2,1)} %broadcast_in_dim.42), calls=%async_computation | async-start | bytes 2097152 | tf_op jit(solution)/shard_map/all_to_all | solution.py:183
  9.0 1.0 %copy-start = (bf16[2,16,64,64]{3,2,1,0:T(8,128)(2,1)S(1)}, bf16[2,16,64,64]{3,2,1,0:T(8,128)(2,1)}, u32[]{:S(2)}) copy-start(bf16[2,16,64,64]{3,2,1,0:T(8,128)(2,1)} %trans.1) | copy-start | bytes 786436
  10.1 0.7 copy-start.4
  24.1 18.0 %all-to-all-start.2 = ((bf16[16,80,128]{2,1,0:T(8,128)(2,1)}), bf16[16,80,128]{2,1,0:T(8,128)(2,1)S(1)}, u32[]{:S(2)}, u32[]{:S(2)}) async-start(bf16[16,80,128]{2,1,0:T(8,128)(2,1)} %shard_map.120), calls=%async_computation.2 | async-start | bytes 655360 | tf_op jit(solution)/shard_map/all_to_all | solution.py:179
  31.9 40.3 %collective-permute-start = (bf16[8,32,16,128]{3,2,1,0:T(8,128)(2,1)S(1)}, bf16[8,32,16,128]{3,2,1,0:T(8,128)(2,1)}, u32[]{:S(2)}, u32[]{:S(2)}) collective-permute-start(bf16[8,32,16,128]{3,2,1,0:T(8,128)(2,1)S(1)} %all-to-all-done.everyone.own), channel_id=1, source_target_pairs={{0,8},{8,0},{16,24},{24,16},{32,40},{40,32},{48,56},{56,48},{64,72... | collective-permute-start | bytes 3145736 | tf_op jit(solution)/shard_map/ppermute | solution.py:206
  32.3 39.9 %collective-permute-start.1 = (bf16[8,32,16,128]{3,2,1,0:T(8,128)(2,1)S(1)}, bf16[8,32,16,128]{3,2,1,0:T(8,128)(2,1)}, u32[]{:S(2)}, u32[]{:S(2)}) collective-permute-start(bf16[8,32,16,128]{3,2,1,0:T(8,128)(2,1)S(1)} %all-to-all-done.everyone.own), channel_id=1, source_target_pairs={{8,16},{24,32},{40,48},{56,64},{72,80},{88,96},{104,112},{16,8},{3... | collective-permute-start | bytes 3145736 | tf_op jit(solution)/shard_map/ppermute | solution.py:208
  35.2 0.9 copy-start.3
  36.1 1.0 %copy-start.6 = (bf16[2,32,32,128]{3,2,1,0:T(8,128)(2,1)S(1)}, bf16[2,32,32,128]{3,2,1,0:T(8,128)(2,1)}, u32[]{:S(2)}) copy-start(bf16[2,32,32,128]{3,2,1,0:T(8,128)(2,1)} %radiation.1) | copy-start | bytes 1572868
  37.1 1.0 %copy-start.7 = (bf16[2,32,32,128]{3,2,1,0:T(8,128)(2,1)S(1)}, bf16[2,32,32,128]{3,2,1,0:T(8,128)(2,1)}, u32[]{:S(2)}) copy-start(bf16[2,32,32,128]{3,2,1,0:T(8,128)(2,1)} %receive.1) | copy-start | bytes 1572868
  42.1 0.7 copy-start.1
  42.8 23.3 %all-to-all-start.1 = ((bf16[16,64,128]{2,1,0:T(8,128)(2,1)}), bf16[16,64,128]{2,1,0:T(8,128)(2,1)S(1)}, u32[]{:S(2)}, u32[]{:S(2)}) async-start(bf16[16,64,128]{2,1,0:T(8,128)(2,1)} %shard_map.119), calls=%async_computation.1 | async-start | bytes 524288 | tf_op jit(solution)/shard_map/all_to_all | solution.py:209
  49.2 1.0 copy-start.2
  67.5 14.3 %all-to-all-start.3 = ((bf16[16,64,128]{2,1,0:T(8,128)(2,1)}), bf16[16,64,128]{2,1,0:T(8,128)(2,1)S(1)}, u32[]{:S(2)}, u32[]{:S(2)}) async-start(bf16[16,64,128]{2,1,0:T(8,128)(2,1)} %shard_map.122), calls=%async_computation.3 | async-start | bytes 524288 | tf_op jit(solution)/shard_map/all_to_all | solution.py:213
  72.2 2.2 %copy-start.5 = (bf16[2,32,2,128,128]{4,3,2,1,0:T(8,128)(2,1)S(1)}, bf16[2,32,2,128,128]{4,3,2,1,0:T(8,128)(2,1)}, u32[]{:S(2)}) copy-start(bf16[2,32,2,128,128]{4,3,2,1,0:T(8,128)(2,1)} %blocks.1) | copy-start | bytes 12582916

commit v2 on v1

v2 whole, which is shorter than its diff:
```python
import jax
import jax.numpy as jnp
from jax import lax
from jax.experimental import pallas as pl
from jax.experimental.pallas import tpu as pltpu
from jax.sharding import PartitionSpec as P

BF = jnp.bfloat16
F32 = jnp.float32
NT = (((1,), (1,)), ((), ()))
NN = (((1,), (0,)), ((), ()))
TN = (((0,), (0,)), ((), ()))
VMEM = pl.BlockSpec(memory_space=pltpu.VMEM)
ANY = pl.BlockSpec(memory_space=pl.ANY)
SMEM = pl.BlockSpec(memory_space=pltpu.SMEM)


def dot(a, b, dims):
    return lax.dot_general(a, b, dims, preferred_element_type=F32)


def params(mib):
    return pltpu.CompilerParams(vmem_limit_bytes=mib * 2**20)


def turn_lanes(x):
    lane = lax.broadcasted_iota(jnp.int32, x.shape, 1)
    return jnp.where(lane % 16 < 8, -pltpu.roll(x, 120, 1), pltpu.roll(x, 8, 1))


def turn_rows(x):
    y = x.reshape(8, 2, 8, x.shape[1])
    return jnp.stack([-y[:, 1], y[:, 0]], axis=1).reshape(x.shape)


def mask_kernel(size, currents, copies, own, alive):
    lane = lax.broadcasted_iota(jnp.int32, (16, 128), 1)
    for c in range(32):
        both = jnp.concatenate([currents[0, c], currents[1, c]], axis=0).astype(F32)
        alive[c] = jnp.where(lane < size[c], 1.0, 0.0)
        both = jnp.where(lane < size[c], both, 0.0).astype(BF)
        own[c] = both
        for d in range(8):
            copies[d, c] = both


def pack_kernel(trans, live, ids, out, rows):
    for pp in range(8):
        for r in range(2):
            tiles = []
            for p in (2 * pp, 2 * pp + 1):
                tile = trans[r, p].astype(F32).T
                tiles.append(jnp.where(live[pl.ds(p, 1), :] == 1, tile, 0.0))
            rows[pl.ds(r * 8 + pp, 64, stride=16), :] = jnp.concatenate(tiles, axis=1)
    out[:, 0:64, :] = rows[...].reshape(16, 64, 128).astype(BF)
    pairs = ids[...].astype(F32)
    pairs = jnp.concatenate([pairs, jnp.zeros((8, 128), F32)], axis=0).astype(BF)
    out[:, 64:80, :] = jnp.broadcast_to(pairs[None], (16, 16, 128))


def weights_kernel(packed, out, rows, ids, sums):
    rows[...] = packed[:, 64:128, :].astype(F32).reshape(1024, 128)
    ids[...] = packed[:, 128:144, :].astype(F32)[:, 0:8, :].reshape(128, 128)
    lane = lax.broadcasted_iota(jnp.int32, (8, 128), 1)
    source = lax.broadcasted_iota(jnp.int32, (256, 128), 0).astype(BF)
    none = jnp.zeros((16, 128), BF)

    def step(i, carry):
        left, hits = [], []
        for n in range(2):
            k = 2 * i + n
            factors = rows[pl.ds((k // 8) * 64 + k % 8, 8, stride=8), :]
            both = jnp.concatenate(
                [jnp.where(lane < 64, factors, 0.0), jnp.where(lane < 64, 0.0, factors)], axis=0
            ).astype(BF)
            left.append(jnp.concatenate([none] * n + [both] + [none] * (1 - n), axis=1))
            hit = source == jnp.broadcast_to(ids[pl.ds(k, 1), :].astype(BF), (256, 128))
            hits.append(jnp.where(hit, jnp.ones((), BF), jnp.zeros((), BF)))
        made = dot(jnp.concatenate(left, axis=0), jnp.concatenate(hits, axis=1), NT)
        for b in range(4):
            for h in range(2):
                sums[h, pl.ds(4 * i + b, 8, stride=256), :] = made[
                    b * 8 : b * 8 + 8, h * 128 : h * 128 + 128
                ]
        return carry

    lax.fori_loop(0, 64, step, 0, unroll=8)
    out[...] = sums[...].astype(BF)


def fold_kernel(radiation, receive, phase, interp, up, down):
    turned = jnp.concatenate([phase[...], jnp.zeros((32, 64), F32)], axis=1).T[0:64]
    cosine = jnp.cos(turned)
    sine = jnp.sin(turned)
    raise4 = []
    for n in range(4):
        left = [jnp.zeros((32, 64 * n), F32)] if n else []
        right = [jnp.zeros((32, 64 * (3 - n)), F32)] if n < 3 else []
        raise4.append(jnp.concatenate(left + [interp[...]] + right, axis=1))
    raise4 = jnp.concatenate(raise4, axis=0).T.astype(BF)
    for g in range(8):
        sent = [dot(raise4, radiation[r, g * 4 : g * 4 + 4].reshape(128, 128), NN) for r in range(2)]
        got = [dot(raise4, receive[r, g * 4 : g * 4 + 4].reshape(128, 128), NN) for r in range(2)]
        for n in range(4):
            c = g * 4 + n
            co = jnp.broadcast_to(cosine[:, c : c + 1], (64, 128))
            si = jnp.broadcast_to(sine[:, c : c + 1], (64, 128))
            ur, ui = (s[n * 64 : n * 64 + 64] for s in sent)
            vr, vi = (s[n * 64 : n * 64 + 64] for s in got)
            b = (c % 2) * 128
            up[c // 2, 0:64, b : b + 128] = (co * ur - si * ui).astype(BF)
            up[c // 2, 64:128, b : b + 128] = (si * ur + co * ui).astype(BF)
            down[c, :, 0:128] = (co * vr + si * vi).astype(BF)
            down[c, :, 128:256] = (co * vi - si * vr).astype(BF)


def parents_kernel(everyone, up, packed, out, rows):
    out[:, 64:144, :] = packed[...]
    for p in range(16):
        x = jnp.concatenate(
            [everyone[:, 2 * p + b].reshape(128, 128) for b in range(2)], axis=1
        )
        y = dot(up[p], x, NT)
        rows[pl.ds(p, 64, stride=16), :] = y[0:64] + turn_lanes(y[64:128])
    out[:, 0:64, :] = rows[...].reshape(16, 64, 128).astype(BF)


def translate_kernel(sources, weights, out):
    for q in range(4):
        src = sources[:, q * 16 : q * 16 + 16, :].reshape(256, 128)
        w = slice(q * 512, q * 512 + 512)
        z = dot(weights[0, w, :], src[0:128], NN) + dot(weights[1, w, :], src[128:256], NN)
        done = z[0:256] + turn_lanes(z[256:512])
        out[:, q * 16 : q * 16 + 16, :] = done.reshape(16, 16, 128).astype(BF)


def near_kernel(place, offset, live, own, partner, far0, far1, far2, far3, blocks, out, far):
    first = place[0] * 32
    even = place[0] % 2 == 0
    bases = (first, jnp.where(even, first + 32, first - 32), jnp.where(even, first - 32, first + 32))
    for k, part in enumerate((far0, far1, far2, far3)):
        for b in range(2):
            far[2 * ((place[2] // 2 + 4 - k) % 4) + (place[2] + b) % 2] = part[b]

    def step(c, carry):
        picked = []
        for j in range(2):
            source = jnp.clip(first + c + offset[c, j], 0, place[1] * 32 - 1)
            x = jnp.zeros((128, 128), BF)
            for cells, base in zip((own, partner, far), bases):
                spot = source - base
                here = (live[c, j] == 1) & (spot >= 0) & (spot < 32)
                x = jnp.where(here, cells[:, jnp.clip(spot, 0, 31)].reshape(128, 128), x)
            picked.append(x)
        parts = [jnp.concatenate([blocks[r, c, j] for j in range(2)], axis=1) for r in range(2)]
        y = dot(jnp.concatenate(picked, axis=1), jnp.concatenate(parts, axis=0), NT)
        out[c] = (y[:, 0:128] + turn_rows(y[:, 128:256])).astype(BF)
        return carry

    lax.fori_loop(0, 32, step, 0, unroll=4)


def far_kernel(translated, down, near, out, rows):
    rows[...] = translated[...].astype(F32).reshape(1024, 128)
    for p in range(16):
        t = rows[pl.ds(p, 64, stride=16), :].T.astype(BF)
        for c in (2 * p, 2 * p + 1):
            y = dot(t, down[c], NN)
            field = y[:, 0:128] + turn_rows(y[:, 128:256]) + near[c].astype(F32)
            out[:, c] = field.reshape(8, 16, 128).astype(BF)


def total_kernel(shares, alive, out):
    total = shares[0].astype(F32)
    for d in range(1, 8):
        total += shares[d].astype(F32)
    total = jnp.where(alive[...] > 0.0, total, 0.0)
    for r in range(2):
        out[r] = total[:, r * 8 : r * 8 + 8].astype(BF)


def call(kernel, shape, scratch, mib, specs, cost, dtype=BF, alias={}):
    many = isinstance(shape, list)
    shapes = shape if many else [shape]
    types = dtype if isinstance(dtype, tuple) else (dtype,) * len(shapes)
    outs = [jax.ShapeDtypeStruct(s, d) for s, d in zip(shapes, types)]
    return pl.pallas_call(
        kernel,
        out_shape=outs if many else outs[0],
        in_specs=specs,
        out_specs=[VMEM] * len(outs) if many else VMEM,
        scratch_shapes=scratch,
        compiler_params=params(mib),
        input_output_aliases=alias,
        cost_estimate=pl.CostEstimate(flops=cost[0], bytes_accessed=cost[1], transcendentals=0),
    )


def local(
    currents,
    cluster_size,
    radiation,
    receive,
    phase,
    interp,
    trans,
    far_ids,
    far_live,
    near_blocks,
    near_offset,
    near_live,
):
    place = lax.axis_index("clus")
    count = lax.axis_size("clus")

    packed = call(
        pack_kernel, (16, 80, 128), [pltpu.VMEM((1024, 128), F32)], 8, [VMEM] * 3, (1, 2**20)
    )(trans, far_live, far_ids.reshape(8, 128))

    alive = lax.broadcasted_iota(jnp.int32, (32, 128), 1) < cluster_size[:, None]
    own = jnp.where(alive[None, :, None, :], currents, jnp.zeros((), BF))
    own = own.transpose(1, 0, 2, 3).reshape(1, 32, 16, 128)
    copies = jnp.broadcast_to(own, (8, 32, 16, 128))
    alive = jnp.broadcast_to(alive[:, None, :].astype(F32), (32, 16, 128))
    everyone = lax.all_to_all(copies, "dir", 0, 0)
    across = [(i, i + 1) for i in range(1, count - 1, 2)]
    across = across + [(b, a) for a, b in across]
    own = own.reshape(32, 16, 128)
    met = [
        lax.ppermute(own, ("clus", "dir"), [(a * 8 + i, b * 8 + (i ^ k)) for a, b in across for i in range(8)])
        for k in range(2)
    ]

    up, down = call(
        fold_kernel, [(16, 128, 256), (32, 64, 256)], [], 12, [VMEM] * 4, (2**31, 2**23)
    )(radiation, receive, phase, interp[0].T)

    everyone, up, down, packed = lax.optimization_barrier((everyone, up, down, packed))
    rows = pltpu.VMEM((1024, 128), F32)
    parents = call(parents_kernel, (16, 144, 128), [rows], 12, [VMEM] * 3, (2**27, 2**21))(
        everyone, up, packed
    )
    partner = lax.ppermute(everyone, "clus", [(i, i ^ 1) for i in range(count)])
    parents, met = lax.optimization_barrier((parents, met))
    far0 = jnp.stack(met)
    far1, far2, far3 = (
        lax.ppermute(far0, "dir", [(i, (i + 2 * k) % 8) for i in range(8)]) for k in (1, 2, 3)
    )
    sources = lax.all_to_all(parents, "clus", 0, 0)
    weights = call(
        weights_kernel,
        (2, 2048, 128),
        [
            pltpu.VMEM((1024, 128), F32),
            pltpu.VMEM((128, 128), F32),
            pltpu.VMEM((2, 2048, 128), F32),
        ],
        12,
        [VMEM],
        (2**32, 2**23),
    )(sources)
    translated = call(translate_kernel, (16, 64, 128), [], 12, [VMEM] * 2, (2**28, 2**21))(
        sources, weights
    )
    back = lax.all_to_all(translated, "clus", 0, 0)
    spots = jnp.stack([place, count, lax.axis_index("dir")]).astype(jnp.int32)
    near = call(
        near_kernel,
        (32, 128, 128),
        [pltpu.VMEM((8, 32, 16, 128), BF)],
        12,
        [SMEM] * 3 + [VMEM] * 7,
        (2**30, 2**23),
    )(spots, near_offset, near_live, everyone, partner, far0, far1, far2, far3, near_blocks)
    partial = call(far_kernel, (8, 32, 16, 128), [rows], 12, [VMEM] * 3, (2**28, 2**22))(
        back, down, near
    )
    shares = lax.all_to_all(partial, "dir", 0, 0)
    return call(total_kernel, (2, 32, 8, 128), [], 8, [VMEM] * 2, (1, 2**21))(shares, alive)


def solution(mesh):
    in_specs = (
        P(None, "clus", "dir", None),
        P("clus"),
        P(None, "clus", "dir", None),
        P(None, "clus", "dir", None),
        P("clus", "dir"),
        P("dir", None, None),
        P(None, "clus", None, "dir"),
        P("clus", None),
        P("clus", None),
        P(None, "clus", "dir", None, None),
        P("clus", "dir"),
        P("clus", "dir"),
    )
    out_specs = P(None, "clus", "dir", None)
    return jax.shard_map(local, mesh=mesh, in_specs=in_specs, out_specs=out_specs, check_vma=False)
```

time: 102 us -> 90.2 us (0.88)
  waiting for transfers between devices: 26.9 us -> 17 us
  local copies, waits for them, and re-layouts: 12.4 us -> 10.8 us
  starting transfers between devices: 26.3 us -> 24.8 us
  other arithmetic: 2.07 us -> 3.48 us
    all_to_all x2 -> x1, starting transfers between devices: 13.2 us -> 5.41 us  [local(): everyone = lax.all_to_all(copies, 'dir', 0, 0)]
    all_to_all x2 -> x1, waiting for transfers between devices: 13.7 us -> 8.24 us  [local(): everyone = lax.all_to_all(copies, 'dir', 0, 0)]
    ppermute x1 -> x5, starting transfers between devices: 1.64 us -> 7.01 us  [the longest x3 4.39 us: local(): lax.ppermute(far0, 'dir', [(i, (i + 2 * k) % 8) for i in range(8)])]
    all_to_all x1, waiting for transfers between devices: 11.5 us -> 7.25 us  [local(): sources = lax.all_to_all(parents, 'clus', 0, 0)]
    all_to_all x1, starting transfers between devices: 6.39 us -> 7.76 us  [local(): sources = lax.all_to_all(parents, 'clus', 0, 0)]
    unnamed x27 -> x28, local copies, waits for them, and re-layouts: 8.87 us -> 8.02 us
    pallas_call x6 -> x7, Pallas kernels: 11.1 us -> 10.6 us  [the longest x1 3.94 us: local(): call(near_kernel, (32, 128, 128), [pltpu.VMEM((8, 32, 16, 128), BF)], 12,...]
  transfers between devices with their start and end apart: 6 -> 9, of which waited for: 4 -> 3; matrix products, arithmetic and copies ran while one was open for 2% -> 2% of each run, Pallas kernels for 15% -> 13%
where the time goes in v2:
time: 90.2 us; the launch traced here: 89.5 us
  starting transfers between devices  24.8 us (27%)
  blocking collectives  18.7 us (21%)
  waiting for transfers between devices  17 us (19%)
  Pallas kernels  14.6 us (16%)
  local copies, waits for them, and re-layouts  10.8 us (12%)
  other arithmetic  3.48 us (4%)
    all_to_all x1, blocking collectives, local(): shares = lax.all_to_all(partial, 'dir', 0, 0)  18.7 us
    all_to_all x1, waiting for transfers between devices, local(): everyone = lax.all_to_all(copies, 'dir', 0, 0)  8.24 us
    unnamed x28, local copies, waits for them, and re-layouts  8.02 us
    all_to_all x1, starting transfers between devices, local(): sources = lax.all_to_all(parents, 'clus', 0, 0)  7.76 us
    all_to_all x1, waiting for transfers between devices, local(): sources = lax.all_to_all(parents, 'clus', 0, 0)  7.25 us
    all_to_all x1, starting transfers between devices, local(): everyone = lax.all_to_all(copies, 'dir', 0, 0)  5.41 us
    ppermute x3, starting transfers between devices, local(): lax.ppermute(far0, 'dir', [(i, (i + 2 * k) % 8) for i in range(8)])  4.39 us
    all_to_all x1, starting transfers between devices, local(): back = lax.all_to_all(translated, 'clus', 0, 0)  4.2 us
  transfers between devices with their start and end apart: 9, of which 3 were waited for; matrix products, arithmetic and copies ran while one was open for 2% of the time, Pallas kernels for 13%

profile of v2, /device:TPU:0, one launch (start us, length us, event | category | flops | bytes accessed | tf_op | source)
XLA Modules:
  0.0 89.5 jit_solution(11988195492009156122)
XLA Ops:
  0.0 0.8 fusion
  0.8 1.6 %copy_bitcast_fusion = bf16[32,16,128]{2,1,0:T(8,128)(2,1)} fusion(bf16[2,32,8,128]{3,2,1,0:T(8,128)(2,1)} %param.12, pred[32,128]{1,0:T(8,128)(4,1)S(1)} %get-tuple-element.24), kind=kLoop, calls=%fused_computation.1 | loop fusion | flops 65536 | bytes 266240 | tf_op jit(solution)/shard_map/broadcast_in_dim | solution.py:223
  2.4 2.0 %broadcast_in_dim.30 = bf16[8,32,16,128]{3,2,1,0:T(8,128)(2,1)} broadcast(bf16[32,16,128]{2,1,0:T(8,128)(2,1)} %copy_bitcast_fusion), dimensions={1,2,3} | broadcast | bytes 1179648 | tf_op jit(solution)/shard_map/broadcast_in_dim | solution.py:223
  4.4 5.4 %all-to-all-start = ((bf16[8,32,16,128]{3,2,1,0:T(8,128)(2,1)}), bf16[8,32,16,128]{3,2,1,0:T(8,128)(2,1)S(1)}, u32[]{:S(2)}, u32[]{:S(2)}) async-start(bf16[8,32,16,128]{3,2,1,0:T(8,128)(2,1)} %broadcast_in_dim.30), calls=%async_computation | async-start | bytes 2097152 | tf_op jit(solution)/shard_map/all_to_all | solution.py:225
  9.8 1.3 %collective-permute-start = (bf16[32,16,128]{2,1,0:T(8,128)(2,1)}, bf16[32,16,128]{2,1,0:T(8,128)(2,1)}, u32[]{:S(2)}, u32[]{:S(2)}) collective-permute-start(bf16[32,16,128]{2,1,0:T(8,128)(2,1)} %copy_bitcast_fusion), channel_id=1, source_target_pairs={{8,16},{9,17},{10,18},{11,19},{12,20},{13,21},{14,22},{15,23},{24,... | collective-permute-start | bytes 393224 | tf_op jit(solution)/shard_map/ppermute | solution.py:230
  11.1 1.3 %collective-permute-start.1 = (bf16[32,16,128]{2,1,0:T(8,128)(2,1)}, bf16[32,16,128]{2,1,0:T(8,128)(2,1)}, u32[]{:S(2)}, u32[]{:S(2)}) collective-permute-start(bf16[32,16,128]{2,1,0:T(8,128)(2,1)} %copy_bitcast_fusion), channel_id=1, source_target_pairs={{8,17},{9,16},{10,19},{11,18},{12,21},{13,20},{14,23},{15,22},{24,... | collective-permute-start | bytes 393224 | tf_op jit(solution)/shard_map/ppermute | solution.py:230
  12.5 0.8 reshape.35.ids
  13.2 1.0 %copy-done.3 = bf16[2,16,64,64]{3,2,1,0:T(8,128)(2,1)S(1)} copy-done((bf16[2,16,64,64]{3,2,1,0:T(8,128)(2,1)S(1)}, bf16[2,16,64,64]{3,2,1,0:T(8,128)(2,1)}, u32[]{:S(2)}) %copy-start.3) | copy-done | bytes 262168
  14.3 0.7 copy-done.6
  15.0 0.4 shard_map.119.packed
  15.4 0.0 copy-done.7
  15.4 0.0 copy-done.8
  15.4 0.0 copy-done.9
  15.5 1.0 %shard_map.118 = (bf16[16,128,256]{2,1,0:T(8,128)(2,1)S(1)}, bf16[32,64,256]{2,1,0:T(8,128)(2,1)S(1)}) custom-call(bf16[2,32,32,128]{3,2,1,0:T(8,128)(2,1)S(1)} %copy-done.7, bf16[2,32,32,128]{3,2,1,0:T(8,128)(2,1)S(1)} %copy-done.8, f32[32,64]{1,0:T(8,128)S(1)} %copy-done.9, f32[32,64]{1,0:T(8,128)S(1)} %bitcast.12), custom_call_target="tpu_custom_call" | custom-call | flops 2147483648 | bytes 8388608 | tf_op jit(solution)/shard_map/pallas_call | solution.py:234
  16.4 1.0 %copy-done.1 = bf16[32,64,256]{2,1,0:T(8,128)(2,1)} copy-done((bf16[32,64,256]{2,1,0:T(8,128)(2,1)}, bf16[32,64,256]{2,1,0:T(8,128)(2,1)S(1)}, u32[]{:S(2)}) %copy-start.1) | copy-done | bytes 1048600
  17.4 8.2 %all-to-all-done.everyone.own = bf16[8,32,16,128]{3,2,1,0:T(8,128)(2,1)S(1)} async-done(((bf16[8,32,16,128]{3,2,1,0:T(8,128)(2,1)}), bf16[8,32,16,128]{3,2,1,0:T(8,128)(2,1)S(1)}, u32[]{:S(2)}, u32[]{:S(2)}) %all-to-all-start) | async-done | bytes 1048608 | tf_op jit(solution)/shard_map/all_to_all | solution.py:225
  25.7 1.4 %shard_map.120 = bf16[16,144,128]{2,1,0:T(8,128)(2,1)} custom-call(bf16[8,32,16,128]{3,2,1,0:T(8,128)(2,1)S(1)} %all-to-all-done.everyone.own, bf16[16,128,256]{2,1,0:T(8,128)(2,1)S(1)} %get-tuple-element.17.up, bf16[16,80,128]{2,1,0:T(8,128)(2,1)S(1)} %shard_map.119.packed), custom_call_target="tpu_custom_call" | custom-call | flops 134217728 | bytes 2097152 | tf_op jit(solution)/shard_map/pallas_call | solution.py:240
  27.1 0.0 collective-permute-done
  27.1 0.0 collective-permute-done.1
  27.1 7.8 %all-to-all-start.1 = ((bf16[16,144,128]{2,1,0:T(8,128)(2,1)}), bf16[16,144,128]{2,1,0:T(8,128)(2,1)S(1)}, u32[]{:S(2)}, u32[]{:S(2)}) async-start(bf16[16,144,128]{2,1,0:T(8,128)(2,1)} %shard_map.120), calls=%async_computation.1 | async-start | bytes 1179648 | tf_op jit(solution)/shard_map/all_to_all | solution.py:249
  34.9 0.4 collective-permute-start.2
  35.3 1.0 %pad_maximum_fusion.far0 = bf16[2,32,16,128]{3,2,1,0:T(8,128)(2,1)S(1)} fusion(bf16[1,32,16,128]{3,2,1,0:T(8,128)(2,1)} %bitcast.7, bf16[1,32,16,128]{3,2,1,0:T(8,128)(2,1)} %bitcast.6), kind=kLoop, calls=%fused_computation | loop fusion | flops 131072 | bytes 524288 | tf_op jit(solution)/shard_map/stack | solution.py:245
  36.3 0.0 copy-start.11
  36.3 0.0 copy-start.12
  36.3 0.6 collective-permute-start.3
  36.9 2.1 %collective-permute-start.4 = (bf16[2,32,16,128]{3,2,1,0:T(8,128)(2,1)S(1)}, bf16[2,32,16,128]{3,2,1,0:T(8,128)(2,1)}, u32[]{:S(2)}, u32[]{:S(2)}) collective-permute-start(bf16[2,32,16,128]{3,2,1,0:T(8,128)(2,1)S(1)} %pad_maximum_fusion.far0), channel_id=1, source_target_pairs={{0,4},{1,5},{2,6},{3,7},{4,0},{5,1},{6,2},{7,3},{8,12},{9,13},{10,... | collective-permute-start | bytes 786440 | tf_op jit(solution)/shard_map/ppermute | solution.py:247
  39.0 1.7 %collective-permute-start.5 = (bf16[2,32,16,128]{3,2,1,0:T(8,128)(2,1)S(1)}, bf16[2,32,16,128]{3,2,1,0:T(8,128)(2,1)}, u32[]{:S(2)}, u32[]{:S(2)}) collective-permute-start(bf16[2,32,16,128]{3,2,1,0:T(8,128)(2,1)S(1)} %pad_maximum_fusion.far0), channel_id=1, source_target_pairs={{0,6},{1,7},{2,0},{3,1},{4,2},{5,3},{6,4},{7,5},{8,14},{9,15},{10,... | collective-permute-start | bytes 786440 | tf_op jit(solution)/shard_map/ppermute | solution.py:247
  40.7 7.2 %all-to-all-done.1.packed.sources = bf16[16,144,128]{2,1,0:T(8,128)(2,1)S(1)} async-done(((bf16[16,144,128]{2,1,0:T(8,128)(2,1)}), bf16[16,144,128]{2,1,0:T(8,128)(2,1)S(1)}, u32[]{:S(2)}, u32[]{:S(2)}) %all-to-all-start.1) | async-done | bytes 589856 | tf_op jit(solution)/shard_map/all_to_all | solution.py:249
  47.9 3.9 %shard_map.121.weights = bf16[2,2048,128]{2,1,0:T(8,128)(2,1)S(1)} custom-call(bf16[16,144,128]{2,1,0:T(8,128)(2,1)S(1)} %all-to-all-done.1.packed.sources), custom_call_target="tpu_custom_call" | custom-call | flops 4294967296 | bytes 8388608 | tf_op jit(solution)/shard_map/pallas_call | solution.py:250
  51.9 1.3 %shard_map.122 = bf16[16,64,128]{2,1,0:T(8,128)(2,1)} custom-call(bf16[16,144,128]{2,1,0:T(8,128)(2,1)S(1)} %all-to-all-done.1.packed.sources, bf16[2,2048,128]{2,1,0:T(8,128)(2,1)S(1)} %shard_map.121.weights), custom_call_target="tpu_custom_call" | custom-call | flops 268435456 | bytes 2097152 | tf_op jit(solution)/shard_map/pallas_call | solution.py:262
  53.2 4.2 %all-to-all-start.2 = ((bf16[16,64,128]{2,1,0:T(8,128)(2,1)}), bf16[16,64,128]{2,1,0:T(8,128)(2,1)}, u32[]{:S(2)}, u32[]{:S(2)}) async-start(bf16[16,64,128]{2,1,0:T(8,128)(2,1)} %shard_map.122), calls=%async_computation.2 | async-start | bytes 524288 | tf_op jit(solution)/shard_map/all_to_all | solution.py:265
  57.4 0.1 copy.14.offset
  57.5 0.1 copy.15.live
  57.6 0.1 pad_add_fusion.place
  57.7 0.0 collective-permute-done.3.far1
  57.7 0.7 copy-done.4
  58.4 0.0 collective-permute-done.4.far2
  58.4 0.0 collective-permute-done.5.far3
  58.4 0.0 collective-permute-done.2.partner
  58.4 0.0 copy-start
  58.4 2.2 %copy-done = bf16[2,32,2,128,128]{4,3,2,1,0:T(8,128)(2,1)S(1)} copy-done((bf16[2,32,2,128,128]{4,3,2,1,0:T(8,128)(2,1)S(1)}, bf16[2,32,2,128,128]{4,3,2,1,0:T(8,128)(2,1)}, u32[]{:S(2)}) %copy-start) | copy-done | bytes 4194328
  60.6 0.9 %copy-done.5 = bf16[2,32,16,128]{3,2,1,0:T(8,128)(2,1)S(1)} copy-done((bf16[2,32,16,128]{3,2,1,0:T(8,128)(2,1)S(1)}, bf16[2,32,16,128]{3,2,1,0:T(8,128)(2,1)}, u32[]{:S(2)}) %copy-start.5) | copy-done | bytes 262168
  61.5 3.9 %shard_map.123.near = bf16[32,128,128]{2,1,0:T(8,128)(2,1)S(1)} custom-call(s32[3]{0:T(128)S(1)} %pad_add_fusion.place, s32[32,2]{1,0:T(8,128)S(1)} %copy.14.offset, s32[32,2]{1,0:T(8,128)S(1)} %copy.15.live, bf16[8,32,16,128]{3,2,1,0:T(8,128)(2,1)S(1)} %all-to-all-done.everyone.own, bf16[8,32,16,128]{3,2,1,0:T(8,128)(2,1)S(1)} %collective-permute-done.2.partner, ...), custom_call_target="tpu_custom_call" | custom-call | flops 1073741824 | bytes 8388608 | tf_op jit(solution)/shard_map/pallas_call | solution.py:267
  65.5 1.5 %all-to-all-done.2.translated = bf16[16,64,128]{2,1,0:T(8,128)(2,1)} async-done(((bf16[16,64,128]{2,1,0:T(8,128)(2,1)}), bf16[16,64,128]{2,1,0:T(8,128)(2,1)}, u32[]{:S(2)}, u32[]{:S(2)}) %all-to-all-start.2) | async-done | bytes 262176 | tf_op jit(solution)/shard_map/all_to_all | solution.py:265
  67.0 1.2 %copy-done.2 = bf16[32,64,256]{2,1,0:T(8,128)(2,1)S(1)} copy-done((bf16[32,64,256]{2,1,0:T(8,128)(2,1)S(1)}, bf16[32,64,256]{2,1,0:T(8,128)(2,1)}, u32[]{:S(2)}) %copy-start.2) | copy-done | bytes 1048600
  68.2 1.8 %shard_map.124 = bf16[8,32,16,128]{3,2,1,0:T(8,128)(2,1)S(1)} custom-call(bf16[16,64,128]{2,1,0:T(8,128)(2,1)} %all-to-all-done.2.translated, bf16[32,64,256]{2,1,0:T(8,128)(2,1)S(1)} %copy-done.2, bf16[32,128,128]{2,1,0:T(8,128)(2,1)S(1)} %shard_map.123.near), custom_call_target="tpu_custom_call" | custom-call | flops 268435456 | bytes 4194304 | tf_op jit(solution)/shard_map/pallas_call | solution.py:275
  70.0 18.7 %all_to_all.20.shares = bf16[8,32,16,128]{3,2,1,0:T(8,128)(2,1)S(1)} all-to-all(bf16[8,32,16,128]{3,2,1,0:T(8,128)(2,1)S(1)} %shard_map.124), channel_id=1, replica_groups=mesh['clus'=16,'dir'=8] {'dir'}, dimensions={0} | all-to-all | bytes 2097152 | tf_op jit(solution)/shard_map/all_to_all | solution.py:278
  88.7 0.8 shard_map.125
  (14 shorter events, 0.0 us)
Async XLA Ops:
  0.0 15.4 %copy-start.7 = (bf16[2,32,32,128]{3,2,1,0:T(8,128)(2,1)S(1)}, bf16[2,32,32,128]{3,2,1,0:T(8,128)(2,1)}, u32[]{:S(2)}) copy-start(bf16[2,32,32,128]{3,2,1,0:T(8,128)(2,1)} %radiation.1) | copy-start | bytes 1572868
  0.0 15.4 %copy-start.8 = (bf16[2,32,32,128]{3,2,1,0:T(8,128)(2,1)S(1)}, bf16[2,32,32,128]{3,2,1,0:T(8,128)(2,1)}, u32[]{:S(2)}) copy-start(bf16[2,32,32,128]{3,2,1,0:T(8,128)(2,1)} %receive.1) | copy-start | bytes 1572868
  0.0 15.4 %copy-start.9 = (f32[32,64]{1,0:T(8,128)S(1)}, f32[32,64]{1,0:T(8,128)}, u32[]{:S(2)}) copy-start(f32[32,64]{1,0:T(8,128)} %phase.1) | copy-start | bytes 24580
  0.0 15.4 %copy-start.10 = (f32[1,64,32]{1,2,0:T(8,128)S(1)}, f32[1,64,32]{1,2,0:T(8,128)}, u32[]{:S(2)}) copy-start(f32[1,64,32]{1,2,0:T(8,128)} %param.17) | copy-start | bytes 24580
  4.4 21.3 %all-to-all-start = ((bf16[8,32,16,128]{3,2,1,0:T(8,128)(2,1)}), bf16[8,32,16,128]{3,2,1,0:T(8,128)(2,1)S(1)}, u32[]{:S(2)}, u32[]{:S(2)}) async-start(bf16[8,32,16,128]{3,2,1,0:T(8,128)(2,1)} %broadcast_in_dim.30), calls=%async_computation | async-start | bytes 2097152 | tf_op jit(solution)/shard_map/all_to_all | solution.py:225
  9.8 17.3 %collective-permute-start = (bf16[32,16,128]{2,1,0:T(8,128)(2,1)}, bf16[32,16,128]{2,1,0:T(8,128)(2,1)}, u32[]{:S(2)}, u32[]{:S(2)}) collective-permute-start(bf16[32,16,128]{2,1,0:T(8,128)(2,1)} %copy_bitcast_fusion), channel_id=1, source_target_pairs={{8,16},{9,17},{10,18},{11,19},{12,20},{13,21},{14,22},{15,23},{24,... | collective-permute-start | bytes 393224 | tf_op jit(solution)/shard_map/ppermute | solution.py:230
  11.1 16.0 %collective-permute-start.1 = (bf16[32,16,128]{2,1,0:T(8,128)(2,1)}, bf16[32,16,128]{2,1,0:T(8,128)(2,1)}, u32[]{:S(2)}, u32[]{:S(2)}) collective-permute-start(bf16[32,16,128]{2,1,0:T(8,128)(2,1)} %copy_bitcast_fusion), channel_id=1, source_target_pairs={{8,17},{9,16},{10,19},{11,18},{12,21},{13,20},{14,23},{15,22},{24,... | collective-permute-start | bytes 393224 | tf_op jit(solution)/shard_map/ppermute | solution.py:230
  13.2 1.0 %copy-start.3 = (bf16[2,16,64,64]{3,2,1,0:T(8,128)(2,1)S(1)}, bf16[2,16,64,64]{3,2,1,0:T(8,128)(2,1)}, u32[]{:S(2)}) copy-start(bf16[2,16,64,64]{3,2,1,0:T(8,128)(2,1)} %trans.1) | copy-start | bytes 786436
  14.3 0.7 copy-start.6
  16.4 1.0 %copy-start.1 = (bf16[32,64,256]{2,1,0:T(8,128)(2,1)}, bf16[32,64,256]{2,1,0:T(8,128)(2,1)S(1)}, u32[]{:S(2)}) copy-start(bf16[32,64,256]{2,1,0:T(8,128)(2,1)S(1)} %get-tuple-element.20.down) | copy-start | bytes 3145732
  27.1 20.8 %all-to-all-start.1 = ((bf16[16,144,128]{2,1,0:T(8,128)(2,1)}), bf16[16,144,128]{2,1,0:T(8,128)(2,1)S(1)}, u32[]{:S(2)}, u32[]{:S(2)}) async-start(bf16[16,144,128]{2,1,0:T(8,128)(2,1)} %shard_map.120), calls=%async_computation.1 | async-start | bytes 1179648 | tf_op jit(solution)/shard_map/all_to_all | solution.py:249
  34.9 23.5 %collective-permute-start.2 = (bf16[8,32,16,128]{3,2,1,0:T(8,128)(2,1)S(1)}, bf16[8,32,16,128]{3,2,1,0:T(8,128)(2,1)S(1)}, u32[]{:S(2)}, u32[]{:S(2)}) collective-permute-start(bf16[8,32,16,128]{3,2,1,0:T(8,128)(2,1)S(1)} %all-to-all-done.everyone.own), channel_id=1, source_target_pairs={{0,8},{8,0},{16,24},{24,16},{32,40},{40,32},{48,56},{56,48},{64,72... | collective-permute-start | bytes 3145736 | tf_op jit(solution)/shard_map/ppermute | solution.py:243
  36.3 21.1 %copy-start.11 = (s32[32,2]{0,1:T(2,128)S(1)}, s32[32,2]{0,1:T(2,128)}, u32[]{:S(2)}) copy-start(s32[32,2]{0,1:T(2,128)} %param.22) | copy-start | bytes 772
  36.3 21.2 %copy-start.12 = (s32[32,2]{0,1:T(2,128)S(1)}, s32[32,2]{0,1:T(2,128)}, u32[]{:S(2)}) copy-start(s32[32,2]{0,1:T(2,128)} %param.23) | copy-start | bytes 772
  36.3 21.4 %collective-permute-start.3 = (bf16[2,32,16,128]{3,2,1,0:T(8,128)(2,1)S(1)}, bf16[2,32,16,128]{3,2,1,0:T(8,128)(2,1)S(1)}, u32[]{:S(2)}, u32[]{:S(2)}) collective-permute-start(bf16[2,32,16,128]{3,2,1,0:T(8,128)(2,1)S(1)} %pad_maximum_fusion.far0), channel_id=1, source_target_pairs={{0,2},{1,3},{2,4},{3,5},{4,6},{5,7},{6,0},{7,1},{8,10},{9,11},{10,... | collective-permute-start | bytes 786440 | tf_op jit(solution)/shard_map/ppermute | solution.py:247
  36.9 21.5 %collective-permute-start.4 = (bf16[2,32,16,128]{3,2,1,0:T(8,128)(2,1)S(1)}, bf16[2,32,16,128]{3,2,1,0:T(8,128)(2,1)}, u32[]{:S(2)}, u32[]{:S(2)}) collective-permute-start(bf16[2,32,16,128]{3,2,1,0:T(8,128)(2,1)S(1)} %pad_maximum_fusion.far0), channel_id=1, source_target_pairs={{0,4},{1,5},{2,6},{3,7},{4,0},{5,1},{6,2},{7,3},{8,12},{9,13},{10,... | collective-permute-start | bytes 786440 | tf_op jit(solution)/shard_map/ppermute | solution.py:247
  39.0 19.4 %collective-permute-start.5 = (bf16[2,32,16,128]{3,2,1,0:T(8,128)(2,1)S(1)}, bf16[2,32,16,128]{3,2,1,0:T(8,128)(2,1)}, u32[]{:S(2)}, u32[]{:S(2)}) collective-permute-start(bf16[2,32,16,128]{3,2,1,0:T(8,128)(2,1)S(1)} %pad_maximum_fusion.far0), channel_id=1, source_target_pairs={{0,6},{1,7},{2,0},{3,1},{4,2},{5,3},{6,4},{7,5},{8,14},{9,15},{10,... | collective-permute-start | bytes 786440 | tf_op jit(solution)/shard_map/ppermute | solution.py:247
  53.2 13.8 %all-to-all-start.2 = ((bf16[16,64,128]{2,1,0:T(8,128)(2,1)}), bf16[16,64,128]{2,1,0:T(8,128)(2,1)}, u32[]{:S(2)}, u32[]{:S(2)}) async-start(bf16[16,64,128]{2,1,0:T(8,128)(2,1)} %shard_map.122), calls=%async_computation.2 | async-start | bytes 524288 | tf_op jit(solution)/shard_map/all_to_all | solution.py:265
  57.7 0.7 copy-start.4
  58.4 2.2 %copy-start = (bf16[2,32,2,128,128]{4,3,2,1,0:T(8,128)(2,1)S(1)}, bf16[2,32,2,128,128]{4,3,2,1,0:T(8,128)(2,1)}, u32[]{:S(2)}) copy-start(bf16[2,32,2,128,128]{4,3,2,1,0:T(8,128)(2,1)} %blocks.1) | copy-start | bytes 12582916
  60.6 0.9 %copy-start.5 = (bf16[2,32,16,128]{3,2,1,0:T(8,128)(2,1)S(1)}, bf16[2,32,16,128]{3,2,1,0:T(8,128)(2,1)}, u32[]{:S(2)}) copy-start(bf16[2,32,16,128]{3,2,1,0:T(8,128)(2,1)} %copy-done.4) | copy-start | bytes 786436
  67.0 1.2 %copy-start.2 = (bf16[32,64,256]{2,1,0:T(8,128)(2,1)S(1)}, bf16[32,64,256]{2,1,0:T(8,128)(2,1)}, u32[]{:S(2)}) copy-start(bf16[32,64,256]{2,1,0:T(8,128)(2,1)} %copy-done.1) | copy-start | bytes 3145732

commit v3 on v2

--- a/solution.py
+++ b/solution.py
@@ -58,14 +58,14 @@
     out[:, 64:80, :] = jnp.broadcast_to(pairs[None], (16, 16, 128))
 
 
-def weights_kernel(packed, out, rows, ids, sums):
+def translate_kernel(packed, out, rows, ids, sums):
     rows[...] = packed[:, 64:128, :].astype(F32).reshape(1024, 128)
     ids[...] = packed[:, 128:144, :].astype(F32)[:, 0:8, :].reshape(128, 128)
     lane = lax.broadcasted_iota(jnp.int32, (8, 128), 1)
-    source = lax.broadcasted_iota(jnp.int32, (256, 128), 0).astype(BF)
+    source = lax.broadcasted_iota(jnp.int32, (128, 128), 1).astype(F32)
+    columns = ids[...].T
     none = jnp.zeros((16, 128), BF)
-
-    def step(i, carry):
+    for i in range(64):
         left, hits = [], []
         for n in range(2):
             k = 2 * i + n
@@ -74,21 +74,24 @@
                 [jnp.where(lane < 64, factors, 0.0), jnp.where(lane < 64, 0.0, factors)], axis=0
             ).astype(BF)
             left.append(jnp.concatenate([none] * n + [both] + [none] * (1 - n), axis=1))
-            hit = source == jnp.broadcast_to(ids[pl.ds(k, 1), :].astype(BF), (256, 128))
-            hits.append(jnp.where(hit, jnp.ones((), BF), jnp.zeros((), BF)))
-        made = dot(jnp.concatenate(left, axis=0), jnp.concatenate(hits, axis=1), NT)
+            wanted = jnp.broadcast_to(columns[:, k : k + 1], (128, 128))
+            halves = [jnp.where(source == wanted - 128.0 * h, 1.0, 0.0).astype(BF) for h in range(2)]
+            hits.append(jnp.concatenate(halves, axis=1))
+        made = dot(jnp.concatenate(left, axis=0), jnp.concatenate(hits, axis=0), NN)
         for b in range(4):
             for h in range(2):
                 sums[h, pl.ds(4 * i + b, 8, stride=256), :] = made[
                     b * 8 : b * 8 + 8, h * 128 : h * 128 + 128
                 ]
-        return carry
-
-    lax.fori_loop(0, 64, step, 0, unroll=8)
-    out[...] = sums[...].astype(BF)
-
-
-def fold_kernel(radiation, receive, phase, interp, up, down):
+    for q in range(4):
+        src = packed[:, q * 16 : q * 16 + 16, :].reshape(256, 128)
+        w = slice(q * 512, q * 512 + 512)
+        z = dot(sums[0, w, :].astype(BF), src[0:128], NN) + dot(sums[1, w, :].astype(BF), src[128:256], NN)
+        done = z[0:256] + turn_lanes(z[256:512])
+        out[:, q * 16 : q * 16 + 16, :] = done.reshape(16, 16, 128).astype(BF)
+
+
+def fold_kernel(patterns, phase, interp, up, down):
     turned = jnp.concatenate([phase[...], jnp.zeros((32, 64), F32)], axis=1).T[0:64]
     cosine = jnp.cos(turned)
     sine = jnp.sin(turned)
@@ -99,8 +102,8 @@
         raise4.append(jnp.concatenate(left + [interp[...]] + right, axis=1))
     raise4 = jnp.concatenate(raise4, axis=0).T.astype(BF)
     for g in range(8):
-        sent = [dot(raise4, radiation[r, g * 4 : g * 4 + 4].reshape(128, 128), NN) for r in range(2)]
-        got = [dot(raise4, receive[r, g * 4 : g * 4 + 4].reshape(128, 128), NN) for r in range(2)]
+        sent = [dot(raise4, patterns[0, r, g * 4 : g * 4 + 4].reshape(128, 128), NN) for r in range(2)]
+        got = [dot(raise4, patterns[1, r, g * 4 : g * 4 + 4].reshape(128, 128), NN) for r in range(2)]
         for n in range(4):
             c = g * 4 + n
             co = jnp.broadcast_to(cosine[:, c : c + 1], (64, 128))
@@ -114,6 +117,11 @@
             down[c, :, 128:256] = (co * vi - si * vr).astype(BF)
 
 
+def pair_kernel(first, second, out):
+    out[0] = first[...]
+    out[1] = second[...]
+
+
 def parents_kernel(everyone, up, packed, out, rows):
     out[:, 64:144, :] = packed[...]
     for p in range(16):
@@ -125,15 +133,6 @@
     out[:, 0:64, :] = rows[...].reshape(16, 64, 128).astype(BF)
 
 
-def translate_kernel(sources, weights, out):
-    for q in range(4):
-        src = sources[:, q * 16 : q * 16 + 16, :].reshape(256, 128)
-        w = slice(q * 512, q * 512 + 512)
-        z = dot(weights[0, w, :], src[0:128], NN) + dot(weights[1, w, :], src[128:256], NN)
-        done = z[0:256] + turn_lanes(z[256:512])
-        out[:, q * 16 : q * 16 + 16, :] = done.reshape(16, 16, 128).astype(BF)
-
-
 def near_kernel(place, offset, live, own, partner, far0, far1, far2, far3, blocks, out, far):
     first = place[0] * 32
     even = place[0] % 2 == 0
@@ -145,11 +144,11 @@
     def step(c, carry):
         picked = []
         for j in range(2):
-            source = jnp.clip(first + c + offset[c, j], 0, place[1] * 32 - 1)
+            source = jnp.clip(first + c + offset[j, c], 0, place[1] * 32 - 1)
             x = jnp.zeros((128, 128), BF)
             for cells, base in zip((own, partner, far), bases):
                 spot = source - base
-                here = (live[c, j] == 1) & (spot >= 0) & (spot < 32)
+                here = (live[j, c] == 1) & (spot >= 0) & (spot < 32)
                 x = jnp.where(here, cells[:, jnp.clip(spot, 0, 31)].reshape(128, 128), x)
             picked.append(x)
         parts = [jnp.concatenate([blocks[r, c, j] for j in range(2)], axis=1) for r in range(2)]
@@ -222,6 +221,8 @@
     own = own.transpose(1, 0, 2, 3).reshape(1, 32, 16, 128)
     copies = jnp.broadcast_to(own, (8, 32, 16, 128))
     alive = jnp.broadcast_to(alive[:, None, :].astype(F32), (32, 16, 128))
+    spots = jnp.stack([place, count, lax.axis_index("dir")]).astype(jnp.int32)
+    copies, spots = lax.optimization_barrier((copies, spots))
     everyone = lax.all_to_all(copies, "dir", 0, 0)
     across = [(i, i + 1) for i in range(1, count - 1, 2)]
     across = across + [(b, a) for a, b in across]
@@ -232,8 +233,8 @@
     ]
 
     up, down = call(
-        fold_kernel, [(16, 128, 256), (32, 64, 256)], [], 12, [VMEM] * 4, (2**31, 2**23)
-    )(radiation, receive, phase, interp[0].T)
+        fold_kernel, [(16, 128, 256), (32, 64, 256)], [], 12, [VMEM] * 3, (2**31, 2**23)
+    )(jnp.stack([radiation, receive]), phase, interp[0].T)
 
     everyone, up, down, packed = lax.optimization_barrier((everyone, up, down, packed))
     rows = pltpu.VMEM((1024, 128), F32)
@@ -242,14 +243,14 @@
     )
     partner = lax.ppermute(everyone, "clus", [(i, i ^ 1) for i in range(count)])
     parents, met = lax.optimization_barrier((parents, met))
-    far0 = jnp.stack(met)
+    far0 = call(pair_kernel, (2, 32, 16, 128), [], 4, [VMEM] * 2, (1, 2**20))(*met)
     far1, far2, far3 = (
         lax.ppermute(far0, "dir", [(i, (i + 2 * k) % 8) for i in range(8)]) for k in (1, 2, 3)
     )
     sources = lax.all_to_all(parents, "clus", 0, 0)
-    weights = call(
-        weights_kernel,
-        (2, 2048, 128),
+    translated = call(
+        translate_kernel,
+        (16, 64, 128),
         [
             pltpu.VMEM((1024, 128), F32),
             pltpu.VMEM((128, 128), F32),
@@ -259,11 +260,7 @@
         [VMEM],
         (2**32, 2**23),
     )(sources)
-    translated = call(translate_kernel, (16, 64, 128), [], 12, [VMEM] * 2, (2**28, 2**21))(
-        sources, weights
-    )
     back = lax.all_to_all(translated, "clus", 0, 0)
-    spots = jnp.stack([place, count, lax.axis_index("dir")]).astype(jnp.int32)
     near = call(
         near_kernel,
         (32, 128, 128),
@@ -271,7 +268,7 @@
         12,
         [SMEM] * 3 + [VMEM] * 7,
         (2**30, 2**23),
-    )(spots, near_offset, near_live, everyone, partner, far0, far1, far2, far3, near_blocks)
+    )(spots, near_offset.T, near_live.T, everyone, partner, far0, far1, far2, far3, near_blocks)
     partial = call(far_kernel, (8, 32, 16, 128), [rows], 12, [VMEM] * 3, (2**28, 2**22))(
         back, down, near
     )

time: 90.2 us -> 87.5 us (0.970)
  waiting for transfers between devices: 17 us -> 19.5 us
  other arithmetic: 3.48 us -> 1.94 us
  starting transfers between devices: 24.8 us -> 23.4 us
  Pallas kernels: 14.6 us -> 13.4 us
  local copies, waits for them, and re-layouts: 10.8 us -> 9.72 us
    ppermute x2, starting transfers between devices: 2.62 us -> 1.33 us  [local(): lax.ppermute(own, ('clus', 'dir'), [(a * 8 + i, b * 8 + (i ^ k)) for a, b...]
    all_to_all x1, waiting for transfers between devices: 8.24 us -> 9.41 us  [local(): everyone = lax.all_to_all(copies, 'dir', 0, 0)]
    pallas_call x3, Pallas kernels: 6.22 us -> 5.1 us  [the longest x1 4.11 us: local(): call(translate_kernel, (16, 64, 128), [pltpu.VMEM((1024, 128), F32), pltp...]
    all_to_all x1, waiting for transfers between devices: 7.25 us -> 8.33 us  [local(): sources = lax.all_to_all(parents, 'clus', 0, 0)]
    unnamed x28 -> x26, local copies, waits for them, and re-layouts: 8.02 us -> 7.83 us
  transfers between devices with their start and end apart: 9 -> 9, of which waited for: 3 -> 3; matrix products, arithmetic and copies ran while one was open for 2% -> 1% of each run, Pallas kernels for 13% -> 12%
where the time goes in v3:
time: 87.5 us; the launch traced here: 86.8 us
  starting transfers between devices  23.4 us (27%)
  waiting for transfers between devices  19.5 us (22%)
  blocking collectives  18.6 us (21%)
  Pallas kernels  13.4 us (15%)
  local copies, waits for them, and re-layouts  9.72 us (11%)
  other arithmetic  1.94 us (2%)
    all_to_all x1, blocking collectives, local(): shares = lax.all_to_all(partial, 'dir', 0, 0)  18.6 us
    all_to_all x1, waiting for transfers between devices, local(): everyone = lax.all_to_all(copies, 'dir', 0, 0)  9.41 us
    all_to_all x1, waiting for transfers between devices, local(): sources = lax.all_to_all(parents, 'clus', 0, 0)  8.33 us
    unnamed x26, local copies, waits for them, and re-layouts  7.83 us
    all_to_all x1, starting transfers between devices, local(): sources = lax.all_to_all(parents, 'clus', 0, 0)  7.76 us
    all_to_all x1, starting transfers between devices, local(): everyone = lax.all_to_all(copies, 'dir', 0, 0)  5.41 us
    ppermute x3, starting transfers between devices, local(): lax.ppermute(far0, 'dir', [(i, (i + 2 * k) % 8) for i in range(8)])  4.28 us
    all_to_all x1, starting transfers between devices, local(): back = lax.all_to_all(translated, 'clus', 0, 0)  4.2 us
  transfers between devices with their start and end apart: 9, of which 3 were waited for; matrix products, arithmetic and copies ran while one was open for 1% of the time, Pallas kernels for 12%

profile of v3, /device:TPU:0, one launch (start us, length us, event | category | flops | bytes accessed | tf_op | source)
XLA Modules:
  0.0 86.8 jit_solution(1785785062063715330)
XLA Ops:
  0.0 0.8 fusion
  0.8 0.9 %copy_bitcast_fusion = bf16[32,16,128]{2,1,0:T(8,128)(2,1)S(1)} fusion(bf16[2,32,8,128]{3,2,1,0:T(8,128)(2,1)} %param.12, pred[32,128]{1,0:T(8,128)(4,1)S(1)} %get-tuple-element.28), kind=kLoop, calls=%fused_computation.1 | loop fusion | flops 65536 | bytes 266240 | tf_op jit(solution)/shard_map/broadcast_in_dim | solution.py:222
  1.8 0.1 pad_add_fusion.place
  1.9 1.1 %broadcast_in_dim.30 = bf16[8,32,16,128]{3,2,1,0:T(8,128)(2,1)} broadcast(bf16[32,16,128]{2,1,0:T(8,128)(2,1)S(1)} %copy_bitcast_fusion), dimensions={1,2,3} | broadcast | bytes 1179648 | tf_op jit(solution)/shard_map/broadcast_in_dim | solution.py:222
  3.0 5.4 %all-to-all-start = ((bf16[8,32,16,128]{3,2,1,0:T(8,128)(2,1)}), bf16[8,32,16,128]{3,2,1,0:T(8,128)(2,1)S(1)}, u32[]{:S(2)}, u32[]{:S(2)}) async-start(bf16[8,32,16,128]{3,2,1,0:T(8,128)(2,1)} %broadcast_in_dim.30), calls=%async_computation | async-start | bytes 2097152 | tf_op jit(solution)/shard_map/all_to_all | solution.py:226
  8.4 0.7 collective-permute-start
  9.0 0.7 collective-permute-start.1
  9.7 0.8 reshape.35.ids
  10.5 1.0 %copy-done.3 = bf16[2,16,64,64]{3,2,1,0:T(8,128)(2,1)S(1)} copy-done((bf16[2,16,64,64]{3,2,1,0:T(8,128)(2,1)S(1)}, bf16[2,16,64,64]{3,2,1,0:T(8,128)(2,1)}, u32[]{:S(2)}) %copy-start.3) | copy-done | bytes 262168
  11.5 0.7 copy-done.6
  12.2 0.4 shard_map.119.packed
  12.7 0.0 copy-done.11
  12.7 0.0 copy-done.12
  12.7 0.1 pad_maximum_fusion.patterns
  12.8 0.0 copy-done.9
  12.8 0.0 copy-done.10
  12.8 1.0 %shard_map.118 = (bf16[16,128,256]{2,1,0:T(8,128)(2,1)S(1)}, bf16[32,64,256]{2,1,0:T(8,128)(2,1)S(1)}) custom-call(bf16[2,2,32,32,128]{4,3,2,1,0:T(8,128)(2,1)S(1)} %pad_maximum_fusion.patterns, f32[32,64]{1,0:T(8,128)S(1)} %copy-done.9, f32[32,64]{1,0:T(8,128)S(1)} %bitcast.16), custom_call_target="tpu_custom_call" | custom-call | flops 2147483648 | bytes 8388608 | tf_op jit(solution)/shard_map/pallas_call | solution.py:235
  13.8 0.0 copy-start.1
  13.8 1.0 %copy-done.1 = bf16[32,64,256]{2,1,0:T(8,128)(2,1)} copy-done((bf16[32,64,256]{2,1,0:T(8,128)(2,1)}, bf16[32,64,256]{2,1,0:T(8,128)(2,1)S(1)}, u32[]{:S(2)}) %copy-start.1) | copy-done | bytes 1048600
  14.8 9.4 %all-to-all-done.everyone.own = bf16[8,32,16,128]{3,2,1,0:T(8,128)(2,1)S(1)} async-done(((bf16[8,32,16,128]{3,2,1,0:T(8,128)(2,1)}), bf16[8,32,16,128]{3,2,1,0:T(8,128)(2,1)S(1)}, u32[]{:S(2)}, u32[]{:S(2)}) %all-to-all-start) | async-done | bytes 1048608 | tf_op jit(solution)/shard_map/all_to_all | solution.py:226
  24.2 1.4 %shard_map.120 = bf16[16,144,128]{2,1,0:T(8,128)(2,1)} custom-call(bf16[8,32,16,128]{3,2,1,0:T(8,128)(2,1)S(1)} %all-to-all-done.everyone.own, bf16[16,128,256]{2,1,0:T(8,128)(2,1)S(1)} %get-tuple-element.20.up, bf16[16,80,128]{2,1,0:T(8,128)(2,1)S(1)} %shard_map.119.packed), custom_call_target="tpu_custom_call" | custom-call | flops 134217728 | bytes 2097152 | tf_op jit(solution)/shard_map/pallas_call | solution.py:241
  25.6 0.0 collective-permute-done.first
  25.6 0.0 collective-permute-done.1.second
  25.6 7.8 %all-to-all-start.1 = ((bf16[16,144,128]{2,1,0:T(8,128)(2,1)}), bf16[16,144,128]{2,1,0:T(8,128)(2,1)S(1)}, u32[]{:S(2)}, u32[]{:S(2)}) async-start(bf16[16,144,128]{2,1,0:T(8,128)(2,1)} %shard_map.120), calls=%async_computation.1 | async-start | bytes 1179648 | tf_op jit(solution)/shard_map/all_to_all | solution.py:250
  33.4 0.4 collective-permute-start.2
  33.8 0.0 copy-start.7
  33.8 0.0 copy-start.8
  33.9 0.6 collective-permute-start.3
  34.4 2.1 %collective-permute-start.4 = (bf16[2,32,16,128]{3,2,1,0:T(8,128)(2,1)S(1)}, bf16[2,32,16,128]{3,2,1,0:T(8,128)(2,1)}, u32[]{:S(2)}, u32[]{:S(2)}) collective-permute-start(bf16[2,32,16,128]{3,2,1,0:T(8,128)(2,1)S(1)} %shard_map.122.far0), channel_id=1, source_target_pairs={{0,4},{1,5},{2,6},{3,7},{4,0},{5,1},{6,2},{7,3},{8,12},{9,13},{10,... | collective-permute-start | bytes 786440 | tf_op jit(solution)/shard_map/ppermute | solution.py:248
  36.5 1.7 %collective-permute-start.5 = (bf16[2,32,16,128]{3,2,1,0:T(8,128)(2,1)S(1)}, bf16[2,32,16,128]{3,2,1,0:T(8,128)(2,1)}, u32[]{:S(2)}, u32[]{:S(2)}) collective-permute-start(bf16[2,32,16,128]{3,2,1,0:T(8,128)(2,1)S(1)} %shard_map.122.far0), channel_id=1, source_target_pairs={{0,6},{1,7},{2,0},{3,1},{4,2},{5,3},{6,4},{7,5},{8,14},{9,15},{10,... | collective-permute-start | bytes 786440 | tf_op jit(solution)/shard_map/ppermute | solution.py:248
  38.1 8.3 %all-to-all-done.1.packed = bf16[16,144,128]{2,1,0:T(8,128)(2,1)S(1)} async-done(((bf16[16,144,128]{2,1,0:T(8,128)(2,1)}), bf16[16,144,128]{2,1,0:T(8,128)(2,1)S(1)}, u32[]{:S(2)}, u32[]{:S(2)}) %all-to-all-start.1) | async-done | bytes 589856 | tf_op jit(solution)/shard_map/all_to_all | solution.py:250
  46.5 4.1 %shard_map.121 = bf16[16,64,128]{2,1,0:T(8,128)(2,1)} custom-call(bf16[16,144,128]{2,1,0:T(8,128)(2,1)S(1)} %all-to-all-done.1.packed), custom_call_target="tpu_custom_call" | custom-call | flops 4294967296 | bytes 8388608 | tf_op jit(solution)/shard_map/pallas_call | solution.py:251
  50.6 4.2 %all-to-all-start.2 = ((bf16[16,64,128]{2,1,0:T(8,128)(2,1)}), bf16[16,64,128]{2,1,0:T(8,128)(2,1)}, u32[]{:S(2)}, u32[]{:S(2)}) async-start(bf16[16,64,128]{2,1,0:T(8,128)(2,1)} %shard_map.121), calls=%async_computation.2 | async-start | bytes 524288 | tf_op jit(solution)/shard_map/all_to_all | solution.py:263
  54.8 0.0 collective-permute-done.3.far1
  54.8 0.0 copy-start.4
  54.8 0.7 copy-done.4
  55.5 0.0 collective-permute-done.4.far2
  55.5 0.0 collective-permute-done.5.far3
  55.5 0.0 collective-permute-done.2.partner
  55.5 0.0 copy-start
  55.6 2.2 %copy-done = bf16[2,32,2,128,128]{4,3,2,1,0:T(8,128)(2,1)S(1)} copy-done((bf16[2,32,2,128,128]{4,3,2,1,0:T(8,128)(2,1)S(1)}, bf16[2,32,2,128,128]{4,3,2,1,0:T(8,128)(2,1)}, u32[]{:S(2)}) %copy-start) | copy-done | bytes 4194328
  57.7 0.9 %copy-done.5 = bf16[2,32,16,128]{3,2,1,0:T(8,128)(2,1)S(1)} copy-done((bf16[2,32,16,128]{3,2,1,0:T(8,128)(2,1)S(1)}, bf16[2,32,16,128]{3,2,1,0:T(8,128)(2,1)}, u32[]{:S(2)}) %copy-start.5) | copy-done | bytes 262168
  58.7 3.9 %shard_map.123.near = bf16[32,128,128]{2,1,0:T(8,128)(2,1)S(1)} custom-call(s32[3]{0:T(128)S(1)} %pad_add_fusion.place, s32[2,32]{1,0:T(2,128)S(1)} %bitcast.14, s32[2,32]{1,0:T(2,128)S(1)} %bitcast.15, bf16[8,32,16,128]{3,2,1,0:T(8,128)(2,1)S(1)} %all-to-all-done.everyone.own, bf16[8,32,16,128]{3,2,1,0:T(8,128)(2,1)S(1)} %collective-permute-done.2.partner, ...), custom_call_target="tpu_custom_call" | custom-call | flops 1073741824 | bytes 8388608 | tf_op jit(solution)/shard_map/pallas_call | solution.py:264
  62.6 1.8 %all-to-all-done.2.translated = bf16[16,64,128]{2,1,0:T(8,128)(2,1)} async-done(((bf16[16,64,128]{2,1,0:T(8,128)(2,1)}), bf16[16,64,128]{2,1,0:T(8,128)(2,1)}, u32[]{:S(2)}, u32[]{:S(2)}) %all-to-all-start.2) | async-done | bytes 262176 | tf_op jit(solution)/shard_map/all_to_all | solution.py:263
  64.4 1.2 %copy-done.2 = bf16[32,64,256]{2,1,0:T(8,128)(2,1)S(1)} copy-done((bf16[32,64,256]{2,1,0:T(8,128)(2,1)S(1)}, bf16[32,64,256]{2,1,0:T(8,128)(2,1)}, u32[]{:S(2)}) %copy-start.2) | copy-done | bytes 1048600
  65.6 1.8 %shard_map.124 = bf16[8,32,16,128]{3,2,1,0:T(8,128)(2,1)S(1)} custom-call(bf16[16,64,128]{2,1,0:T(8,128)(2,1)} %all-to-all-done.2.translated, bf16[32,64,256]{2,1,0:T(8,128)(2,1)S(1)} %copy-done.2, bf16[32,128,128]{2,1,0:T(8,128)(2,1)S(1)} %shard_map.123.near), custom_call_target="tpu_custom_call" | custom-call | flops 268435456 | bytes 4194304 | tf_op jit(solution)/shard_map/pallas_call | solution.py:272
  67.3 18.6 %all_to_all.20.shares = bf16[8,32,16,128]{3,2,1,0:T(8,128)(2,1)S(1)} all-to-all(bf16[8,32,16,128]{3,2,1,0:T(8,128)(2,1)S(1)} %shard_map.124), channel_id=1, replica_groups=mesh['clus'=16,'dir'=8] {'dir'}, dimensions={0} | all-to-all | bytes 2097152 | tf_op jit(solution)/shard_map/all_to_all | solution.py:275
  86.0 0.8 shard_map.125
  (12 shorter events, 0.1 us)
Async XLA Ops:
  0.0 12.7 %copy-start.11 = (bf16[2,32,32,128]{3,2,1,0:T(8,128)(2,1)S(1)}, bf16[2,32,32,128]{3,2,1,0:T(8,128)(2,1)}, u32[]{:S(2)}) copy-start(bf16[2,32,32,128]{3,2,1,0:T(8,128)(2,1)} %param.15) | copy-start | bytes 1572868
  0.0 12.7 %copy-start.12 = (bf16[2,32,32,128]{3,2,1,0:T(8,128)(2,1)S(1)}, bf16[2,32,32,128]{3,2,1,0:T(8,128)(2,1)}, u32[]{:S(2)}) copy-start(bf16[2,32,32,128]{3,2,1,0:T(8,128)(2,1)} %param.14) | copy-start | bytes 1572868
  0.0 12.8 %copy-start.9 = (f32[32,64]{1,0:T(8,128)S(1)}, f32[32,64]{1,0:T(8,128)}, u32[]{:S(2)}) copy-start(f32[32,64]{1,0:T(8,128)} %phase.1) | copy-start | bytes 24580
  0.0 12.8 %copy-start.10 = (f32[1,64,32]{1,2,0:T(8,128)S(1)}, f32[1,64,32]{1,2,0:T(8,128)}, u32[]{:S(2)}) copy-start(f32[1,64,32]{1,2,0:T(8,128)} %param.17) | copy-start | bytes 24580
  3.0 21.3 %all-to-all-start = ((bf16[8,32,16,128]{3,2,1,0:T(8,128)(2,1)}), bf16[8,32,16,128]{3,2,1,0:T(8,128)(2,1)S(1)}, u32[]{:S(2)}, u32[]{:S(2)}) async-start(bf16[8,32,16,128]{3,2,1,0:T(8,128)(2,1)} %broadcast_in_dim.30), calls=%async_computation | async-start | bytes 2097152 | tf_op jit(solution)/shard_map/all_to_all | solution.py:226
  8.4 17.3 %collective-permute-start = (bf16[32,16,128]{2,1,0:T(8,128)(2,1)S(1)}, bf16[32,16,128]{2,1,0:T(8,128)(2,1)S(1)}, u32[]{:S(2)}, u32[]{:S(2)}) collective-permute-start(bf16[32,16,128]{2,1,0:T(8,128)(2,1)S(1)} %copy_bitcast_fusion), channel_id=1, source_target_pairs={{8,16},{9,17},{10,18},{11,19},{12,20},{13,21},{14,22},{15,23},{24,... | collective-permute-start | bytes 393224 | tf_op jit(solution)/shard_map/ppermute | solution.py:231
  9.0 16.6 %collective-permute-start.1 = (bf16[32,16,128]{2,1,0:T(8,128)(2,1)S(1)}, bf16[32,16,128]{2,1,0:T(8,128)(2,1)S(1)}, u32[]{:S(2)}, u32[]{:S(2)}) collective-permute-start(bf16[32,16,128]{2,1,0:T(8,128)(2,1)S(1)} %copy_bitcast_fusion), channel_id=1, source_target_pairs={{8,17},{9,16},{10,19},{11,18},{12,21},{13,20},{14,23},{15,22},{24,... | collective-permute-start | bytes 393224 | tf_op jit(solution)/shard_map/ppermute | solution.py:231
  10.5 1.0 %copy-start.3 = (bf16[2,16,64,64]{3,2,1,0:T(8,128)(2,1)S(1)}, bf16[2,16,64,64]{3,2,1,0:T(8,128)(2,1)}, u32[]{:S(2)}) copy-start(bf16[2,16,64,64]{3,2,1,0:T(8,128)(2,1)} %trans.1) | copy-start | bytes 786436
  11.5 0.7 copy-start.6
  13.8 1.0 %copy-start.1 = (bf16[32,64,256]{2,1,0:T(8,128)(2,1)}, bf16[32,64,256]{2,1,0:T(8,128)(2,1)S(1)}, u32[]{:S(2)}) copy-start(bf16[32,64,256]{2,1,0:T(8,128)(2,1)S(1)} %get-tuple-element.23.down) | copy-start | bytes 3145732
  25.6 20.8 %all-to-all-start.1 = ((bf16[16,144,128]{2,1,0:T(8,128)(2,1)}), bf16[16,144,128]{2,1,0:T(8,128)(2,1)S(1)}, u32[]{:S(2)}, u32[]{:S(2)}) async-start(bf16[16,144,128]{2,1,0:T(8,128)(2,1)} %shard_map.120), calls=%async_computation.1 | async-start | bytes 1179648 | tf_op jit(solution)/shard_map/all_to_all | solution.py:250
  33.4 22.1 %collective-permute-start.2 = (bf16[8,32,16,128]{3,2,1,0:T(8,128)(2,1)S(1)}, bf16[8,32,16,128]{3,2,1,0:T(8,128)(2,1)S(1)}, u32[]{:S(2)}, u32[]{:S(2)}) collective-permute-start(bf16[8,32,16,128]{3,2,1,0:T(8,128)(2,1)S(1)} %all-to-all-done.everyone.own), channel_id=1, source_target_pairs={{0,8},{8,0},{16,24},{24,16},{32,40},{40,32},{48,56},{56,48},{64,72... | collective-permute-start | bytes 3145736 | tf_op jit(solution)/shard_map/ppermute | solution.py:244
  33.8 21.7 %copy-start.7 = (s32[32,2]{0,1:T(2,128)S(1)}, s32[32,2]{0,1:T(2,128)}, u32[]{:S(2)}) copy-start(s32[32,2]{0,1:T(2,128)} %param.22) | copy-start | bytes 772
  33.8 21.7 %copy-start.8 = (s32[32,2]{0,1:T(2,128)S(1)}, s32[32,2]{0,1:T(2,128)}, u32[]{:S(2)}) copy-start(s32[32,2]{0,1:T(2,128)} %param.23) | copy-start | bytes 772
  33.9 20.9 %collective-permute-start.3 = (bf16[2,32,16,128]{3,2,1,0:T(8,128)(2,1)S(1)}, bf16[2,32,16,128]{3,2,1,0:T(8,128)(2,1)S(1)}, u32[]{:S(2)}, u32[]{:S(2)}) collective-permute-start(bf16[2,32,16,128]{3,2,1,0:T(8,128)(2,1)S(1)} %shard_map.122.far0), channel_id=1, source_target_pairs={{0,2},{1,3},{2,4},{3,5},{4,6},{5,7},{6,0},{7,1},{8,10},{9,11},{10,... | collective-permute-start | bytes 786440 | tf_op jit(solution)/shard_map/ppermute | solution.py:248
  34.4 21.1 %collective-permute-start.4 = (bf16[2,32,16,128]{3,2,1,0:T(8,128)(2,1)S(1)}, bf16[2,32,16,128]{3,2,1,0:T(8,128)(2,1)}, u32[]{:S(2)}, u32[]{:S(2)}) collective-permute-start(bf16[2,32,16,128]{3,2,1,0:T(8,128)(2,1)S(1)} %shard_map.122.far0), channel_id=1, source_target_pairs={{0,4},{1,5},{2,6},{3,7},{4,0},{5,1},{6,2},{7,3},{8,12},{9,13},{10,... | collective-permute-start | bytes 786440 | tf_op jit(solution)/shard_map/ppermute | solution.py:248
  36.5 19.0 %collective-permute-start.5 = (bf16[2,32,16,128]{3,2,1,0:T(8,128)(2,1)S(1)}, bf16[2,32,16,128]{3,2,1,0:T(8,128)(2,1)}, u32[]{:S(2)}, u32[]{:S(2)}) collective-permute-start(bf16[2,32,16,128]{3,2,1,0:T(8,128)(2,1)S(1)} %shard_map.122.far0), channel_id=1, source_target_pairs={{0,6},{1,7},{2,0},{3,1},{4,2},{5,3},{6,4},{7,5},{8,14},{9,15},{10,... | collective-permute-start | bytes 786440 | tf_op jit(solution)/shard_map/ppermute | solution.py:248
  50.6 13.8 %all-to-all-start.2 = ((bf16[16,64,128]{2,1,0:T(8,128)(2,1)}), bf16[16,64,128]{2,1,0:T(8,128)(2,1)}, u32[]{:S(2)}, u32[]{:S(2)}) async-start(bf16[16,64,128]{2,1,0:T(8,128)(2,1)} %shard_map.121), calls=%async_computation.2 | async-start | bytes 524288 | tf_op jit(solution)/shard_map/all_to_all | solution.py:263
  54.8 0.7 copy-start.4
  55.5 2.2 %copy-start = (bf16[2,32,2,128,128]{4,3,2,1,0:T(8,128)(2,1)S(1)}, bf16[2,32,2,128,128]{4,3,2,1,0:T(8,128)(2,1)}, u32[]{:S(2)}) copy-start(bf16[2,32,2,128,128]{4,3,2,1,0:T(8,128)(2,1)} %blocks.1) | copy-start | bytes 12582916
  57.7 0.9 %copy-start.5 = (bf16[2,32,16,128]{3,2,1,0:T(8,128)(2,1)S(1)}, bf16[2,32,16,128]{3,2,1,0:T(8,128)(2,1)}, u32[]{:S(2)}) copy-start(bf16[2,32,16,128]{3,2,1,0:T(8,128)(2,1)} %copy-done.4) | copy-start | bytes 786436
  64.4 1.2 %copy-start.2 = (bf16[32,64,256]{2,1,0:T(8,128)(2,1)S(1)}, bf16[32,64,256]{2,1,0:T(8,128)(2,1)}, u32[]{:S(2)}) copy-start(bf16[32,64,256]{2,1,0:T(8,128)(2,1)} %copy-done.1) | copy-start | bytes 3145732

commit v4 on v3

--- a/solution.py
+++ b/solution.py
@@ -133,9 +133,15 @@
     out[:, 0:64, :] = rows[...].reshape(16, 64, 128).astype(BF)
 
 
-def near_kernel(place, offset, live, own, partner, far0, far1, far2, far3, blocks, out, far):
+def near_kernel(place, offset, live, own, partner, far0, far1, far2, far3, blocks, out, far, held, ready):
     first = place[0] * 32
     even = place[0] % 2 == 0
+    chunks = [
+        pltpu.make_async_copy(blocks.at[:, pl.ds(g * 8, 8)], held.at[:, pl.ds(g * 8, 8)], ready.at[g])
+        for g in range(4)
+    ]
+    for copy in chunks:
+        copy.start()
     bases = (first, jnp.where(even, first + 32, first - 32), jnp.where(even, first - 32, first + 32))
     for k, part in enumerate((far0, far1, far2, far3)):
         for b in range(2):
@@ -151,12 +157,14 @@
                 here = (live[j, c] == 1) & (spot >= 0) & (spot < 32)
                 x = jnp.where(here, cells[:, jnp.clip(spot, 0, 31)].reshape(128, 128), x)
             picked.append(x)
-        parts = [jnp.concatenate([blocks[r, c, j] for j in range(2)], axis=1) for r in range(2)]
+        parts = [jnp.concatenate([held[r, c, j] for j in range(2)], axis=1) for r in range(2)]
         y = dot(jnp.concatenate(picked, axis=1), jnp.concatenate(parts, axis=0), NT)
         out[c] = (y[:, 0:128] + turn_rows(y[:, 128:256])).astype(BF)
         return carry
 
-    lax.fori_loop(0, 32, step, 0, unroll=4)
+    for g in range(4):
+        chunks[g].wait()
+        lax.fori_loop(g * 8, g * 8 + 8, step, 0, unroll=4)
 
 
 def far_kernel(translated, down, near, out, rows):
@@ -216,11 +224,21 @@
         pack_kernel, (16, 80, 128), [pltpu.VMEM((1024, 128), F32)], 8, [VMEM] * 3, (1, 2**20)
     )(trans, far_live, far_ids.reshape(8, 128))
 
-    alive = lax.broadcasted_iota(jnp.int32, (32, 128), 1) < cluster_size[:, None]
-    own = jnp.where(alive[None, :, None, :], currents, jnp.zeros((), BF))
-    own = own.transpose(1, 0, 2, 3).reshape(1, 32, 16, 128)
-    copies = jnp.broadcast_to(own, (8, 32, 16, 128))
-    alive = jnp.broadcast_to(alive[:, None, :].astype(F32), (32, 16, 128))
+    copies, own, alive = call(
+        mask_kernel,
+        [(8, 32, 16, 128), (32, 16, 128), (32, 16, 128)],
+        [],
+        60,
+        [SMEM, VMEM],
+        (1, 2**21),
+        (BF, BF, F32),
+    )(cluster_size, currents)
+    across = [(i, i + 1) for i in range(1, count - 1, 2)]
+    across = across + [(b, a) for a, b in across]
+    met = [
+        lax.ppermute(own, ("clus", "dir"), [(a * 8 + i, b * 8 + (i ^ k)) for a, b in across for i in range(8)])
+        for k in range(2)
+    ]
     spots = jnp.stack([place, count, lax.axis_index("dir")]).astype(jnp.int32)
     copies, spots = lax.optimization_barrier((copies, spots))
     everyone = lax.all_to_all(copies, "dir", 0, 0)
@@ -264,9 +282,13 @@
     near = call(
         near_kernel,
         (32, 128, 128),
-        [pltpu.VMEM((8, 32, 16, 128), BF)],
-        12,
-        [SMEM] * 3 + [VMEM] * 7,
+        [
+            pltpu.VMEM((8, 32, 16, 128), BF),
+            pltpu.VMEM((2, 32, 2, 128, 128), BF),
+            pltpu.SemaphoreType.DMA((4,)),
+        ],
+        58,
+        [SMEM] * 3 + [VMEM] * 6 + [ANY],
         (2**30, 2**23),
     )(spots, near_offset.T, near_live.T, everyone, partner, far0, far1, far2, far3, near_blocks)
     partial = call(far_kernel, (8, 32, 16, 128), [rows], 12, [VMEM] * 3, (2**28, 2**22))(

time: 87.5 us -> 85.6 us (0.978)
  local copies, waits for them, and re-layouts: 9.72 us -> 4.49 us
  Pallas kernels: 13.4 us -> 18.4 us
  waiting for transfers between devices: 19.5 us -> 18.4 us
    pallas_call x1 -> x2, Pallas kernels: 3.88 us -> 8.87 us  [the longest x1 6.77 us: local(): call(near_kernel, (32, 128, 128), [pltpu.VMEM((8, 32, 16, 128), BF), pltp...]
    unnamed x26 -> x20, local copies, waits for them, and re-layouts: 7.83 us -> 3.73 us
    all_to_all x1, waiting for transfers between devices: 9.41 us -> 7.98 us  [local(): everyone = lax.all_to_all(copies, 'dir', 0, 0)]
    ppermute x2, starting transfers between devices: 1.33 us -> 2.61 us  [local(): lax.ppermute(own, ('clus', 'dir'), [(a * 8 + i, b * 8 + (i ^ k)) for a, b...]
    another operation x1, other arithmetic: 0.1 us -> 1.3 us  [local(): jnp.stack([radiation, receive])]
    broadcast_in_dim x2 -> x0, local copies, waits for them, and re-layouts: 1.12 us -> none  [the longest x1 1.1 us: local(): copies = jnp.broadcast_to(own, (8, 32, 16, 128))]
    ppermute x3, starting transfers between devices: 4.28 us -> 3.21 us  [local(): lax.ppermute(far0, 'dir', [(i, (i + 2 * k) % 8) for i in range(8)])]
    pallas_call x1, Pallas kernels: 0.02 us -> 0.98 us  [local(): call(pair_kernel, (2, 32, 16, 128), [], 4, [VMEM] * 2, (1, 2 ** 20))(*met)]
  transfers between devices with their start and end apart: 9 -> 9, of which waited for: 3 -> 3; matrix products, arithmetic and copies ran while one was open for 1% -> 2% of each run, Pallas kernels for 12% -> 17%
where the time goes in v4:
time: 85.6 us; the launch traced here: 85 us
  starting transfers between devices  22.9 us (27%)
  blocking collectives  18.8 us (22%)
  Pallas kernels  18.4 us (21%)
  waiting for transfers between devices  18.4 us (21%)
  local copies, waits for them, and re-layouts  4.49 us (5%)
  other arithmetic  1.91 us (2%)
    all_to_all x1, blocking collectives, local(): shares = lax.all_to_all(partial, 'dir', 0, 0)  18.8 us
    all_to_all x1, waiting for transfers between devices, local(): sources = lax.all_to_all(parents, 'clus', 0, 0)  8.45 us
    all_to_all x1, waiting for transfers between devices, local(): everyone = lax.all_to_all(copies, 'dir', 0, 0)  7.98 us
    all_to_all x1, starting transfers between devices, local(): sources = lax.all_to_all(parents, 'clus', 0, 0)  7.76 us
    pallas_call x1, Pallas kernels, local(): call(near_kernel, (32, 128, 128), [pltpu.VMEM((8, 32, 16, 128), BF), pltp...  6.77 us
    all_to_all x1, starting transfers between devices, local(): everyone = lax.all_to_all(copies, 'dir', 0, 0)  5.4 us
    pallas_call x1, Pallas kernels, local(): call(translate_kernel, (16, 64, 128), [pltpu.VMEM((1024, 128), F32), pltp...  4.1 us
    unnamed x20, local copies, waits for them, and re-layouts  3.73 us
  transfers between devices with their start and end apart: 9, of which 3 were waited for; matrix products, arithmetic and copies ran while one was open for 2% of the time, Pallas kernels for 17%

profile of v4, /device:TPU:0, one launch (start us, length us, event | category | flops | bytes accessed | tf_op | source)
XLA Modules:
  0.0 85.0 jit_solution(6421099379896927380)
XLA Ops:
  0.0 0.0 copy-start.7
  0.0 0.0 copy-start.6
  0.0 2.1 %shard_map.118 = (bf16[8,32,16,128]{3,2,1,0:T(8,128)(2,1)}, bf16[32,16,128]{2,1,0:T(8,128)(2,1)}, f32[32,16,128]{2,1,0:T(8,128)}) custom-call(s32[32]{0:T(128)} %size.1, bf16[2,32,8,128]{3,2,1,0:T(8,128)(2,1)} %currents.1), custom_call_target="tpu_custom_call" | custom-call | flops 1 | bytes 2097152 | tf_op jit(solution)/shard_map/pallas_call | solution.py:227
  2.1 0.6 pad_add_fusion.place
  2.7 5.4 %all-to-all-start = ((bf16[8,32,16,128]{3,2,1,0:T(8,128)(2,1)}), bf16[8,32,16,128]{3,2,1,0:T(8,128)(2,1)S(1)}, u32[]{:S(2)}, u32[]{:S(2)}) async-start(bf16[8,32,16,128]{3,2,1,0:T(8,128)(2,1)} %get-tuple-element.20), calls=%async_computation | async-start | bytes 2097152 | tf_op jit(solution)/shard_map/all_to_all | solution.py:244
  8.1 1.3 %collective-permute-start.1 = (bf16[32,16,128]{2,1,0:T(8,128)(2,1)}, bf16[32,16,128]{2,1,0:T(8,128)(2,1)}, u32[]{:S(2)}, u32[]{:S(2)}) collective-permute-start(bf16[32,16,128]{2,1,0:T(8,128)(2,1)} %get-tuple-element.26), channel_id=1, source_target_pairs={{8,17},{9,16},{10,19},{11,18},{12,21},{13,20},{14,23},{15,22},{24,... | collective-permute-start | bytes 393224 | tf_op jit(solution)/shard_map/ppermute | solution.py:249
  9.4 1.3 %collective-permute-start = (bf16[32,16,128]{2,1,0:T(8,128)(2,1)}, bf16[32,16,128]{2,1,0:T(8,128)(2,1)}, u32[]{:S(2)}, u32[]{:S(2)}) collective-permute-start(bf16[32,16,128]{2,1,0:T(8,128)(2,1)} %get-tuple-element.26), channel_id=1, source_target_pairs={{8,16},{9,17},{10,18},{11,19},{12,20},{13,21},{14,22},{15,23},{24,... | collective-permute-start | bytes 393224 | tf_op jit(solution)/shard_map/ppermute | solution.py:249
  10.7 0.8 reshape.3.ids
  11.5 0.0 copy-start.3
  11.5 1.0 %copy-done.3 = bf16[2,16,64,64]{3,2,1,0:T(8,128)(2,1)S(1)} copy-done((bf16[2,16,64,64]{3,2,1,0:T(8,128)(2,1)S(1)}, bf16[2,16,64,64]{3,2,1,0:T(8,128)(2,1)}, u32[]{:S(2)}) %copy-start.3) | copy-done | bytes 262168
  12.5 0.0 copy-start.5
  12.5 0.7 copy-done.5
  13.2 0.4 shard_map.120.packed
  13.7 1.3 %pad_maximum_fusion.patterns = bf16[2,2,32,32,128]{4,3,2,1,0:T(8,128)(2,1)S(1)} fusion(bf16[1,2,32,32,128]{4,3,2,1,0:T(8,128)(2,1)} %bitcast.10, bf16[1,2,32,32,128]{4,3,2,1,0:T(8,128)(2,1)} %bitcast.11), kind=kLoop, calls=%fused_computation | loop fusion | flops 524288 | bytes 2097152 | tf_op jit(solution)/shard_map/stack | solution.py:255
  15.0 0.0 copy-done.7
  15.0 0.0 copy-done.6
  15.0 1.0 %shard_map.119 = (bf16[16,128,256]{2,1,0:T(8,128)(2,1)S(1)}, bf16[32,64,256]{2,1,0:T(8,128)(2,1)S(1)}) custom-call(bf16[2,2,32,32,128]{4,3,2,1,0:T(8,128)(2,1)S(1)} %pad_maximum_fusion.patterns, f32[32,64]{1,0:T(8,128)S(1)} %copy-done.6, f32[32,64]{1,0:T(8,128)S(1)} %bitcast.9), custom_call_target="tpu_custom_call" | custom-call | flops 2147483648 | bytes 8388608 | tf_op jit(solution)/shard_map/pallas_call | solution.py:253
  16.0 8.0 %all-to-all-done.everyone.own = bf16[8,32,16,128]{3,2,1,0:T(8,128)(2,1)S(1)} async-done(((bf16[8,32,16,128]{3,2,1,0:T(8,128)(2,1)}), bf16[8,32,16,128]{3,2,1,0:T(8,128)(2,1)S(1)}, u32[]{:S(2)}, u32[]{:S(2)}) %all-to-all-start) | async-done | bytes 1048608 | tf_op jit(solution)/shard_map/all_to_all | solution.py:244
  24.0 1.4 %shard_map.121 = bf16[16,144,128]{2,1,0:T(8,128)(2,1)} custom-call(bf16[8,32,16,128]{3,2,1,0:T(8,128)(2,1)S(1)} %all-to-all-done.everyone.own, bf16[16,128,256]{2,1,0:T(8,128)(2,1)S(1)} %get-tuple-element.24.up, bf16[16,80,128]{2,1,0:T(8,128)(2,1)S(1)} %shard_map.120.packed), custom_call_target="tpu_custom_call" | custom-call | flops 134217728 | bytes 2097152 | tf_op jit(solution)/shard_map/pallas_call | solution.py:259
  25.4 0.0 collective-permute-done.1.second
  25.4 0.0 collective-permute-done.first
  25.4 7.8 %all-to-all-start.1 = ((bf16[16,144,128]{2,1,0:T(8,128)(2,1)}), bf16[16,144,128]{2,1,0:T(8,128)(2,1)S(1)}, u32[]{:S(2)}, u32[]{:S(2)}) async-start(bf16[16,144,128]{2,1,0:T(8,128)(2,1)} %shard_map.121), calls=%async_computation.1 | async-start | bytes 1179648 | tf_op jit(solution)/shard_map/all_to_all | solution.py:268
  33.1 0.4 collective-permute-start.2
  33.5 1.0 %shard_map.123.far0 = bf16[2,32,16,128]{3,2,1,0:T(8,128)(2,1)S(1)} custom-call(bf16[32,16,128]{2,1,0:T(8,128)(2,1)} %collective-permute-done.first, bf16[32,16,128]{2,1,0:T(8,128)(2,1)} %collective-permute-done.1.second), custom_call_target="tpu_custom_call" | custom-call | flops 1 | bytes 1048576 | tf_op jit(solution)/shard_map/pallas_call | solution.py:264
  34.5 0.0 copy-start.2
  34.5 1.2 %collective-permute-start.5 = (bf16[2,32,16,128]{3,2,1,0:T(8,128)(2,1)S(1)}, bf16[2,32,16,128]{3,2,1,0:T(8,128)(2,1)S(1)}, u32[]{:S(2)}, u32[]{:S(2)}) collective-permute-start(bf16[2,32,16,128]{3,2,1,0:T(8,128)(2,1)S(1)} %shard_map.123.far0), channel_id=1, source_target_pairs={{0,6},{1,7},{2,0},{3,1},{4,2},{5,3},{6,4},{7,5},{8,14},{9,15},{10,... | collective-permute-start | bytes 786440 | tf_op jit(solution)/shard_map/ppermute | solution.py:266
  35.7 1.4 %collective-permute-start.4 = (bf16[2,32,16,128]{3,2,1,0:T(8,128)(2,1)S(1)}, bf16[2,32,16,128]{3,2,1,0:T(8,128)(2,1)S(1)}, u32[]{:S(2)}, u32[]{:S(2)}) collective-permute-start(bf16[2,32,16,128]{3,2,1,0:T(8,128)(2,1)S(1)} %shard_map.123.far0), channel_id=1, source_target_pairs={{0,4},{1,5},{2,6},{3,7},{4,0},{5,1},{6,2},{7,3},{8,12},{9,13},{10,... | collective-permute-start | bytes 786440 | tf_op jit(solution)/shard_map/ppermute | solution.py:266
  37.2 0.6 collective-permute-start.3
  37.7 8.4 %all-to-all-done.1.packed = bf16[16,144,128]{2,1,0:T(8,128)(2,1)S(1)} async-done(((bf16[16,144,128]{2,1,0:T(8,128)(2,1)}), bf16[16,144,128]{2,1,0:T(8,128)(2,1)S(1)}, u32[]{:S(2)}, u32[]{:S(2)}) %all-to-all-start.1) | async-done | bytes 589856 | tf_op jit(solution)/shard_map/all_to_all | solution.py:268
  46.2 4.1 %shard_map.122 = bf16[16,64,128]{2,1,0:T(8,128)(2,1)} custom-call(bf16[16,144,128]{2,1,0:T(8,128)(2,1)S(1)} %all-to-all-done.1.packed), custom_call_target="tpu_custom_call" | custom-call | flops 4294967296 | bytes 8388608 | tf_op jit(solution)/shard_map/pallas_call | solution.py:269
  50.3 0.0 copy-done
  50.3 0.0 copy-done.2
  50.3 3.5 %all-to-all-start.2 = ((bf16[16,64,128]{2,1,0:T(8,128)(2,1)}), bf16[16,64,128]{2,1,0:T(8,128)(2,1)S(1)}, u32[]{:S(2)}, u32[]{:S(2)}) async-start(bf16[16,64,128]{2,1,0:T(8,128)(2,1)} %shard_map.122), calls=%async_computation.2 | async-start | bytes 524288 | tf_op jit(solution)/shard_map/all_to_all | solution.py:281
  53.8 0.0 collective-permute-done.5.far3
  53.8 0.0 copy-start.8
  53.9 0.0 collective-permute-done.4.far2
  53.9 0.0 copy-start.9
  53.9 0.0 collective-permute-done.3.far1
  53.9 0.0 collective-permute-done.2.partner
  53.9 0.7 copy-done.8
  54.6 0.1 copy-done.9
  54.6 6.8 %shard_map.124.near = bf16[32,128,128]{2,1,0:T(8,128)(2,1)} custom-call(s32[3]{0:T(128)} %pad_add_fusion.place, s32[2,32]{1,0:T(2,128)} %bitcast.12, s32[2,32]{1,0:T(2,128)} %bitcast.13, bf16[8,32,16,128]{3,2,1,0:T(8,128)(2,1)} %copy-done, bf16[8,32,16,128]{3,2,1,0:T(8,128)(2,1)} %collective-permute-done.2.partner, bf16[2,32,16,128]{3,2,1,0:T(8,128)(2,1)} %copy-done.2, ...), custom_call_target="tpu_custom_call" | custom-call | flops 1073741824 | bytes 8388608 | tf_op jit(solution)/shard_map/pallas_call | solution.py:282
  61.4 1.9 %all-to-all-done.2.translated = bf16[16,64,128]{2,1,0:T(8,128)(2,1)S(1)} async-done(((bf16[16,64,128]{2,1,0:T(8,128)(2,1)}), bf16[16,64,128]{2,1,0:T(8,128)(2,1)S(1)}, u32[]{:S(2)}, u32[]{:S(2)}) %all-to-all-start.2) | async-done | bytes 262176 | tf_op jit(solution)/shard_map/all_to_all | solution.py:281
  63.4 1.2 %copy-done.1 = bf16[32,128,128]{2,1,0:T(8,128)(2,1)S(1)} copy-done((bf16[32,128,128]{2,1,0:T(8,128)(2,1)S(1)}, bf16[32,128,128]{2,1,0:T(8,128)(2,1)}, u32[]{:S(2)}) %copy-start.1) | copy-done | bytes 1048600
  64.6 0.8 shard_map.125
  65.4 18.8 %all_to_all.20.shares = bf16[8,32,16,128]{3,2,1,0:T(8,128)(2,1)S(1)} all-to-all(bf16[8,32,16,128]{3,2,1,0:T(8,128)(2,1)S(1)} %shard_map.125), channel_id=1, replica_groups=mesh['clus'=16,'dir'=8] {'dir'}, dimensions={0} | all-to-all | bytes 2097152 | tf_op jit(solution)/shard_map/all_to_all | solution.py:297
  84.2 0.0 copy-done.4
  84.2 0.8 shard_map.126
  (3 shorter events, 0.0 us)
Async XLA Ops:
  0.0 15.0 %copy-start.7 = (f32[1,64,32]{1,2,0:T(8,128)S(1)}, f32[1,64,32]{1,2,0:T(8,128)}, u32[]{:S(2)}) copy-start(f32[1,64,32]{1,2,0:T(8,128)} %param.17) | copy-start | bytes 24580
  0.0 15.0 %copy-start.6 = (f32[32,64]{1,0:T(8,128)S(1)}, f32[32,64]{1,0:T(8,128)}, u32[]{:S(2)}) copy-start(f32[32,64]{1,0:T(8,128)} %phase.1) | copy-start | bytes 24580
  2.7 21.2 %all-to-all-start = ((bf16[8,32,16,128]{3,2,1,0:T(8,128)(2,1)}), bf16[8,32,16,128]{3,2,1,0:T(8,128)(2,1)S(1)}, u32[]{:S(2)}, u32[]{:S(2)}) async-start(bf16[8,32,16,128]{3,2,1,0:T(8,128)(2,1)} %get-tuple-element.20), calls=%async_computation | async-start | bytes 2097152 | tf_op jit(solution)/shard_map/all_to_all | solution.py:244
  8.1 17.2 %collective-permute-start.1 = (bf16[32,16,128]{2,1,0:T(8,128)(2,1)}, bf16[32,16,128]{2,1,0:T(8,128)(2,1)}, u32[]{:S(2)}, u32[]{:S(2)}) collective-permute-start(bf16[32,16,128]{2,1,0:T(8,128)(2,1)} %get-tuple-element.26), channel_id=1, source_target_pairs={{8,17},{9,16},{10,19},{11,18},{12,21},{13,20},{14,23},{15,22},{24,... | collective-permute-start | bytes 393224 | tf_op jit(solution)/shard_map/ppermute | solution.py:249
  9.4 15.9 %collective-permute-start = (bf16[32,16,128]{2,1,0:T(8,128)(2,1)}, bf16[32,16,128]{2,1,0:T(8,128)(2,1)}, u32[]{:S(2)}, u32[]{:S(2)}) collective-permute-start(bf16[32,16,128]{2,1,0:T(8,128)(2,1)} %get-tuple-element.26), channel_id=1, source_target_pairs={{8,16},{9,17},{10,18},{11,19},{12,20},{13,21},{14,22},{15,23},{24,... | collective-permute-start | bytes 393224 | tf_op jit(solution)/shard_map/ppermute | solution.py:249
  11.5 1.0 %copy-start.3 = (bf16[2,16,64,64]{3,2,1,0:T(8,128)(2,1)S(1)}, bf16[2,16,64,64]{3,2,1,0:T(8,128)(2,1)}, u32[]{:S(2)}) copy-start(bf16[2,16,64,64]{3,2,1,0:T(8,128)(2,1)} %trans.1) | copy-start | bytes 786436
  12.5 0.7 copy-start.5
  24.0 26.3 %copy-start = (bf16[8,32,16,128]{3,2,1,0:T(8,128)(2,1)}, bf16[8,32,16,128]{3,2,1,0:T(8,128)(2,1)S(1)}, u32[]{:S(2)}) copy-start(bf16[8,32,16,128]{3,2,1,0:T(8,128)(2,1)S(1)} %all-to-all-done.everyone.own) | copy-start | bytes 3145732
  25.4 20.8 %all-to-all-start.1 = ((bf16[16,144,128]{2,1,0:T(8,128)(2,1)}), bf16[16,144,128]{2,1,0:T(8,128)(2,1)S(1)}, u32[]{:S(2)}, u32[]{:S(2)}) async-start(bf16[16,144,128]{2,1,0:T(8,128)(2,1)} %shard_map.121), calls=%async_computation.1 | async-start | bytes 1179648 | tf_op jit(solution)/shard_map/all_to_all | solution.py:268
  33.1 20.8 %collective-permute-start.2 = (bf16[8,32,16,128]{3,2,1,0:T(8,128)(2,1)S(1)}, bf16[8,32,16,128]{3,2,1,0:T(8,128)(2,1)}, u32[]{:S(2)}, u32[]{:S(2)}) collective-permute-start(bf16[8,32,16,128]{3,2,1,0:T(8,128)(2,1)S(1)} %all-to-all-done.everyone.own), channel_id=1, source_target_pairs={{0,8},{8,0},{16,24},{24,16},{32,40},{40,32},{48,56},{56,48},{64,72... | collective-permute-start | bytes 3145736 | tf_op jit(solution)/shard_map/ppermute | solution.py:262
  34.5 15.8 %copy-start.2 = (bf16[2,32,16,128]{3,2,1,0:T(8,128)(2,1)}, bf16[2,32,16,128]{3,2,1,0:T(8,128)(2,1)S(1)}, u32[]{:S(2)}) copy-start(bf16[2,32,16,128]{3,2,1,0:T(8,128)(2,1)S(1)} %shard_map.123.far0) | copy-start | bytes 786436
  34.5 19.3 %collective-permute-start.5 = (bf16[2,32,16,128]{3,2,1,0:T(8,128)(2,1)S(1)}, bf16[2,32,16,128]{3,2,1,0:T(8,128)(2,1)S(1)}, u32[]{:S(2)}, u32[]{:S(2)}) collective-permute-start(bf16[2,32,16,128]{3,2,1,0:T(8,128)(2,1)S(1)} %shard_map.123.far0), channel_id=1, source_target_pairs={{0,6},{1,7},{2,0},{3,1},{4,2},{5,3},{6,4},{7,5},{8,14},{9,15},{10,... | collective-permute-start | bytes 786440 | tf_op jit(solution)/shard_map/ppermute | solution.py:266
  35.7 18.1 %collective-permute-start.4 = (bf16[2,32,16,128]{3,2,1,0:T(8,128)(2,1)S(1)}, bf16[2,32,16,128]{3,2,1,0:T(8,128)(2,1)S(1)}, u32[]{:S(2)}, u32[]{:S(2)}) collective-permute-start(bf16[2,32,16,128]{3,2,1,0:T(8,128)(2,1)S(1)} %shard_map.123.far0), channel_id=1, source_target_pairs={{0,4},{1,5},{2,6},{3,7},{4,0},{5,1},{6,2},{7,3},{8,12},{9,13},{10,... | collective-permute-start | bytes 786440 | tf_op jit(solution)/shard_map/ppermute | solution.py:266
  37.2 16.7 %collective-permute-start.3 = (bf16[2,32,16,128]{3,2,1,0:T(8,128)(2,1)S(1)}, bf16[2,32,16,128]{3,2,1,0:T(8,128)(2,1)}, u32[]{:S(2)}, u32[]{:S(2)}) collective-permute-start(bf16[2,32,16,128]{3,2,1,0:T(8,128)(2,1)S(1)} %shard_map.123.far0), channel_id=1, source_target_pairs={{0,2},{1,3},{2,4},{3,5},{4,6},{5,7},{6,0},{7,1},{8,10},{9,11},{10,... | collective-permute-start | bytes 786440 | tf_op jit(solution)/shard_map/ppermute | solution.py:266
  50.3 13.1 %all-to-all-start.2 = ((bf16[16,64,128]{2,1,0:T(8,128)(2,1)}), bf16[16,64,128]{2,1,0:T(8,128)(2,1)S(1)}, u32[]{:S(2)}, u32[]{:S(2)}) async-start(bf16[16,64,128]{2,1,0:T(8,128)(2,1)} %shard_map.122), calls=%async_computation.2 | async-start | bytes 524288 | tf_op jit(solution)/shard_map/all_to_all | solution.py:281
  53.8 0.7 copy-start.8
  53.9 0.8 copy-start.9
  63.4 1.2 %copy-start.1 = (bf16[32,128,128]{2,1,0:T(8,128)(2,1)S(1)}, bf16[32,128,128]{2,1,0:T(8,128)(2,1)}, u32[]{:S(2)}) copy-start(bf16[32,128,128]{2,1,0:T(8,128)(2,1)} %shard_map.124.near) | copy-start | bytes 3145732
  64.6 19.6 %copy-start.4 = (f32[32,16,128]{2,1,0:T(8,128)S(1)}, f32[32,16,128]{2,1,0:T(8,128)}, u32[]{:S(2)}) copy-start(f32[32,16,128]{2,1,0:T(8,128)} %get-tuple-element.32.alive) | copy-start | bytes 786436

commit v5 on v4

--- a/solution.py
+++ b/solution.py
@@ -240,7 +240,6 @@
         for k in range(2)
     ]
     spots = jnp.stack([place, count, lax.axis_index("dir")]).astype(jnp.int32)
-    copies, spots = lax.optimization_barrier((copies, spots))
     everyone = lax.all_to_all(copies, "dir", 0, 0)
     across = [(i, i + 1) for i in range(1, count - 1, 2)]
     across = across + [(b, a) for a, b in across]
@@ -254,7 +253,9 @@
         fold_kernel, [(16, 128, 256), (32, 64, 256)], [], 12, [VMEM] * 3, (2**31, 2**23)
     )(jnp.stack([radiation, receive]), phase, interp[0].T)
 
-    everyone, up, down, packed = lax.optimization_barrier((everyone, up, down, packed))
+    everyone, up, down, packed, spots = lax.optimization_barrier(
+        (everyone, up, down, packed, spots)
+    )
     rows = pltpu.VMEM((1024, 128), F32)
     parents = call(parents_kernel, (16, 144, 128), [rows], 12, [VMEM] * 3, (2**27, 2**21))(
         everyone, up, packed

time: 85.6 us -> 84.9 us (level)
  local copies, waits for them, and re-layouts: 4.49 us -> 3.14 us
    unnamed x20 -> x22, local copies, waits for them, and re-layouts: 3.73 us -> 3.07 us
where the time goes in v5:
time: 84.9 us; the launch traced here: 84.4 us
  starting transfers between devices  22.9 us (27%)
  waiting for transfers between devices  19.1 us (22%)
  blocking collectives  18.7 us (22%)
  Pallas kernels  18.4 us (22%)
  local copies, waits for them, and re-layouts  3.14 us (4%)
  other arithmetic  1.95 us (2%)
    all_to_all x1, blocking collectives, local(): shares = lax.all_to_all(partial, 'dir', 0, 0)  18.7 us
    all_to_all x1, waiting for transfers between devices, local(): everyone = lax.all_to_all(copies, 'dir', 0, 0)  8.67 us
    all_to_all x1, waiting for transfers between devices, local(): sources = lax.all_to_all(parents, 'clus', 0, 0)  8.46 us
    all_to_all x1, starting transfers between devices, local(): sources = lax.all_to_all(parents, 'clus', 0, 0)  7.76 us
    pallas_call x1, Pallas kernels, local(): call(near_kernel, (32, 128, 128), [pltpu.VMEM((8, 32, 16, 128), BF), pltp...  6.78 us
    all_to_all x1, starting transfers between devices, local(): everyone = lax.all_to_all(copies, 'dir', 0, 0)  5.4 us
    pallas_call x1, Pallas kernels, local(): call(translate_kernel, (16, 64, 128), [pltpu.VMEM((1024, 128), F32), pltp...  4.1 us
    all_to_all x1, starting transfers between devices, local(): back = lax.all_to_all(translated, 'clus', 0, 0)  3.53 us
  transfers between devices with their start and end apart: 9, of which 3 were waited for; matrix products, arithmetic and copies ran while one was open for 2% of the time, Pallas kernels for 17%

profile of v5, /device:TPU:0, one launch (start us, length us, event | category | flops | bytes accessed | tf_op | source)
XLA Modules:
  0.0 84.4 jit_solution(881142599345769567)
XLA Ops:
  0.0 0.0 copy-start.7
  0.0 2.1 %shard_map.118 = (bf16[8,32,16,128]{3,2,1,0:T(8,128)(2,1)}, bf16[32,16,128]{2,1,0:T(8,128)(2,1)}, f32[32,16,128]{2,1,0:T(8,128)}) custom-call(s32[32]{0:T(128)} %size.1, bf16[2,32,8,128]{3,2,1,0:T(8,128)(2,1)} %currents.1), custom_call_target="tpu_custom_call" | custom-call | flops 1 | bytes 2097152 | tf_op jit(solution)/shard_map/pallas_call | solution.py:227
  2.1 5.4 %all-to-all-start = ((bf16[8,32,16,128]{3,2,1,0:T(8,128)(2,1)}), bf16[8,32,16,128]{3,2,1,0:T(8,128)(2,1)S(1)}, u32[]{:S(2)}, u32[]{:S(2)}) async-start(bf16[8,32,16,128]{3,2,1,0:T(8,128)(2,1)} %get-tuple-element.18), calls=%async_computation | async-start | bytes 2097152 | tf_op jit(solution)/shard_map/all_to_all | solution.py:243
  7.5 1.3 %collective-permute-start.1 = (bf16[32,16,128]{2,1,0:T(8,128)(2,1)}, bf16[32,16,128]{2,1,0:T(8,128)(2,1)}, u32[]{:S(2)}, u32[]{:S(2)}) collective-permute-start(bf16[32,16,128]{2,1,0:T(8,128)(2,1)} %get-tuple-element.24), channel_id=1, source_target_pairs={{8,17},{9,16},{10,19},{11,18},{12,21},{13,20},{14,23},{15,22},{24,... | collective-permute-start | bytes 393224 | tf_op jit(solution)/shard_map/ppermute | solution.py:248
  8.8 1.3 %collective-permute-start = (bf16[32,16,128]{2,1,0:T(8,128)(2,1)}, bf16[32,16,128]{2,1,0:T(8,128)(2,1)}, u32[]{:S(2)}, u32[]{:S(2)}) collective-permute-start(bf16[32,16,128]{2,1,0:T(8,128)(2,1)} %get-tuple-element.24), channel_id=1, source_target_pairs={{8,16},{9,17},{10,18},{11,19},{12,20},{13,21},{14,22},{15,23},{24,... | collective-permute-start | bytes 393224 | tf_op jit(solution)/shard_map/ppermute | solution.py:248
  10.2 1.3 %pad_maximum_fusion.patterns = bf16[2,2,32,32,128]{4,3,2,1,0:T(8,128)(2,1)S(1)} fusion(bf16[1,2,32,32,128]{4,3,2,1,0:T(8,128)(2,1)} %bitcast.10, bf16[1,2,32,32,128]{4,3,2,1,0:T(8,128)(2,1)} %bitcast.11), kind=kLoop, calls=%fused_computation | loop fusion | flops 524288 | bytes 2097152 | tf_op jit(solution)/shard_map/stack | solution.py:254
  11.5 0.0 copy-start.10
  11.5 0.0 copy-start.5
  11.5 0.0 copy-done.7
  11.5 0.0 copy-done.6
  11.5 1.0 %shard_map.119 = (bf16[16,128,256]{2,1,0:T(8,128)(2,1)S(1)}, bf16[32,64,256]{2,1,0:T(8,128)(2,1)S(1)}) custom-call(bf16[2,2,32,32,128]{4,3,2,1,0:T(8,128)(2,1)S(1)} %pad_maximum_fusion.patterns, f32[32,64]{1,0:T(8,128)S(1)} %copy-done.6, f32[32,64]{1,0:T(8,128)S(1)} %bitcast.9), custom_call_target="tpu_custom_call" | custom-call | flops 2147483648 | bytes 8388608 | tf_op jit(solution)/shard_map/pallas_call | solution.py:252
  12.5 0.0 copy-done.10
  12.5 0.1 reshape.3.ids
  12.6 0.0 copy-done.5
  12.6 1.0 %copy-done.3 = bf16[2,16,64,64]{3,2,1,0:T(8,128)(2,1)S(1)} copy-done((bf16[2,16,64,64]{3,2,1,0:T(8,128)(2,1)S(1)}, bf16[2,16,64,64]{3,2,1,0:T(8,128)(2,1)}, u32[]{:S(2)}) %copy-start.3) | copy-done | bytes 262168
  13.6 0.4 shard_map.120.packed
  14.1 0.7 pad_add_fusion.place
  14.7 8.7 %all-to-all-done.everyone.own = bf16[8,32,16,128]{3,2,1,0:T(8,128)(2,1)S(1)} async-done(((bf16[8,32,16,128]{3,2,1,0:T(8,128)(2,1)}), bf16[8,32,16,128]{3,2,1,0:T(8,128)(2,1)S(1)}, u32[]{:S(2)}, u32[]{:S(2)}) %all-to-all-start) | async-done | bytes 1048608 | tf_op jit(solution)/shard_map/all_to_all | solution.py:243
  23.4 1.4 %shard_map.121 = bf16[16,144,128]{2,1,0:T(8,128)(2,1)} custom-call(bf16[8,32,16,128]{3,2,1,0:T(8,128)(2,1)S(1)} %all-to-all-done.everyone.own, bf16[16,128,256]{2,1,0:T(8,128)(2,1)S(1)} %get-tuple-element.22.up, bf16[16,80,128]{2,1,0:T(8,128)(2,1)S(1)} %shard_map.120.packed), custom_call_target="tpu_custom_call" | custom-call | flops 134217728 | bytes 2097152 | tf_op jit(solution)/shard_map/pallas_call | solution.py:260
  24.8 0.0 collective-permute-done.1.second
  24.8 0.0 collective-permute-done.first
  24.8 7.8 %all-to-all-start.1 = ((bf16[16,144,128]{2,1,0:T(8,128)(2,1)}), bf16[16,144,128]{2,1,0:T(8,128)(2,1)S(1)}, u32[]{:S(2)}, u32[]{:S(2)}) async-start(bf16[16,144,128]{2,1,0:T(8,128)(2,1)} %shard_map.121), calls=%async_computation.1 | async-start | bytes 1179648 | tf_op jit(solution)/shard_map/all_to_all | solution.py:269
  32.6 0.4 collective-permute-start.2
  33.0 1.0 %shard_map.123.far0 = bf16[2,32,16,128]{3,2,1,0:T(8,128)(2,1)S(1)} custom-call(bf16[32,16,128]{2,1,0:T(8,128)(2,1)} %collective-permute-done.first, bf16[32,16,128]{2,1,0:T(8,128)(2,1)} %collective-permute-done.1.second), custom_call_target="tpu_custom_call" | custom-call | flops 1 | bytes 1048576 | tf_op jit(solution)/shard_map/pallas_call | solution.py:265
  33.9 0.0 copy-start.2
  34.0 1.2 %collective-permute-start.5 = (bf16[2,32,16,128]{3,2,1,0:T(8,128)(2,1)S(1)}, bf16[2,32,16,128]{3,2,1,0:T(8,128)(2,1)S(1)}, u32[]{:S(2)}, u32[]{:S(2)}) collective-permute-start(bf16[2,32,16,128]{3,2,1,0:T(8,128)(2,1)S(1)} %shard_map.123.far0), channel_id=1, source_target_pairs={{0,6},{1,7},{2,0},{3,1},{4,2},{5,3},{6,4},{7,5},{8,14},{9,15},{10,... | collective-permute-start | bytes 786440 | tf_op jit(solution)/shard_map/ppermute | solution.py:267
  35.2 1.4 %collective-permute-start.4 = (bf16[2,32,16,128]{3,2,1,0:T(8,128)(2,1)S(1)}, bf16[2,32,16,128]{3,2,1,0:T(8,128)(2,1)S(1)}, u32[]{:S(2)}, u32[]{:S(2)}) collective-permute-start(bf16[2,32,16,128]{3,2,1,0:T(8,128)(2,1)S(1)} %shard_map.123.far0), channel_id=1, source_target_pairs={{0,4},{1,5},{2,6},{3,7},{4,0},{5,1},{6,2},{7,3},{8,12},{9,13},{10,... | collective-permute-start | bytes 786440 | tf_op jit(solution)/shard_map/ppermute | solution.py:267
  36.6 0.6 collective-permute-start.3
  37.2 8.5 %all-to-all-done.1.packed = bf16[16,144,128]{2,1,0:T(8,128)(2,1)S(1)} async-done(((bf16[16,144,128]{2,1,0:T(8,128)(2,1)}), bf16[16,144,128]{2,1,0:T(8,128)(2,1)S(1)}, u32[]{:S(2)}, u32[]{:S(2)}) %all-to-all-start.1) | async-done | bytes 589856 | tf_op jit(solution)/shard_map/all_to_all | solution.py:269
  45.6 4.1 %shard_map.122 = bf16[16,64,128]{2,1,0:T(8,128)(2,1)} custom-call(bf16[16,144,128]{2,1,0:T(8,128)(2,1)S(1)} %all-to-all-done.1.packed), custom_call_target="tpu_custom_call" | custom-call | flops 4294967296 | bytes 8388608 | tf_op jit(solution)/shard_map/pallas_call | solution.py:270
  49.7 0.0 copy-done
  49.7 0.0 copy-done.2
  49.7 3.5 %all-to-all-start.2 = ((bf16[16,64,128]{2,1,0:T(8,128)(2,1)}), bf16[16,64,128]{2,1,0:T(8,128)(2,1)S(1)}, u32[]{:S(2)}, u32[]{:S(2)}) async-start(bf16[16,64,128]{2,1,0:T(8,128)(2,1)} %shard_map.122), calls=%async_computation.2 | async-start | bytes 524288 | tf_op jit(solution)/shard_map/all_to_all | solution.py:282
  53.3 0.0 collective-permute-done.5.far3
  53.3 0.0 copy-start.8
  53.3 0.0 collective-permute-done.4.far2
  53.3 0.0 copy-start.9
  53.3 0.0 collective-permute-done.3.far1
  53.3 0.0 collective-permute-done.2.partner
  53.3 0.7 copy-done.8
  54.0 0.1 copy-done.9
  54.1 6.8 %shard_map.124.near = bf16[32,128,128]{2,1,0:T(8,128)(2,1)} custom-call(s32[3]{0:T(128)} %pad_add_fusion.place, s32[2,32]{1,0:T(2,128)} %bitcast.12, s32[2,32]{1,0:T(2,128)} %bitcast.13, bf16[8,32,16,128]{3,2,1,0:T(8,128)(2,1)} %copy-done, bf16[8,32,16,128]{3,2,1,0:T(8,128)(2,1)} %collective-permute-done.2.partner, bf16[2,32,16,128]{3,2,1,0:T(8,128)(2,1)} %copy-done.2, ...), custom_call_target="tpu_custom_call" | custom-call | flops 1073741824 | bytes 8388608 | tf_op jit(solution)/shard_map/pallas_call | solution.py:283
  60.9 1.9 %all-to-all-done.2.translated = bf16[16,64,128]{2,1,0:T(8,128)(2,1)S(1)} async-done(((bf16[16,64,128]{2,1,0:T(8,128)(2,1)}), bf16[16,64,128]{2,1,0:T(8,128)(2,1)S(1)}, u32[]{:S(2)}, u32[]{:S(2)}) %all-to-all-start.2) | async-done | bytes 262176 | tf_op jit(solution)/shard_map/all_to_all | solution.py:282
  62.8 1.2 %copy-done.1 = bf16[32,128,128]{2,1,0:T(8,128)(2,1)S(1)} copy-done((bf16[32,128,128]{2,1,0:T(8,128)(2,1)S(1)}, bf16[32,128,128]{2,1,0:T(8,128)(2,1)}, u32[]{:S(2)}) %copy-start.1) | copy-done | bytes 1048600
  64.0 0.8 shard_map.125
  64.8 18.7 %all_to_all.20.shares = bf16[8,32,16,128]{3,2,1,0:T(8,128)(2,1)S(1)} all-to-all(bf16[8,32,16,128]{3,2,1,0:T(8,128)(2,1)S(1)} %shard_map.125), channel_id=1, replica_groups=mesh['clus'=16,'dir'=8] {'dir'}, dimensions={0} | all-to-all | bytes 2097152 | tf_op jit(solution)/shard_map/all_to_all | solution.py:298
  83.6 0.0 copy-done.4
  83.6 0.8 shard_map.126
  (5 shorter events, 0.0 us)
Async XLA Ops:
  0.0 11.5 %copy-start.7 = (f32[1,64,32]{1,2,0:T(8,128)S(1)}, f32[1,64,32]{1,2,0:T(8,128)}, u32[]{:S(2)}) copy-start(f32[1,64,32]{1,2,0:T(8,128)} %param.17) | copy-start | bytes 24580
  0.0 11.5 %copy-start.6 = (f32[32,64]{1,0:T(8,128)S(1)}, f32[32,64]{1,0:T(8,128)}, u32[]{:S(2)}) copy-start(f32[32,64]{1,0:T(8,128)} %phase.1) | copy-start | bytes 24580
  2.1 21.2 %all-to-all-start = ((bf16[8,32,16,128]{3,2,1,0:T(8,128)(2,1)}), bf16[8,32,16,128]{3,2,1,0:T(8,128)(2,1)S(1)}, u32[]{:S(2)}, u32[]{:S(2)}) async-start(bf16[8,32,16,128]{3,2,1,0:T(8,128)(2,1)} %get-tuple-element.18), calls=%async_computation | async-start | bytes 2097152 | tf_op jit(solution)/shard_map/all_to_all | solution.py:243
  7.5 17.2 %collective-permute-start.1 = (bf16[32,16,128]{2,1,0:T(8,128)(2,1)}, bf16[32,16,128]{2,1,0:T(8,128)(2,1)}, u32[]{:S(2)}, u32[]{:S(2)}) collective-permute-start(bf16[32,16,128]{2,1,0:T(8,128)(2,1)} %get-tuple-element.24), channel_id=1, source_target_pairs={{8,17},{9,16},{10,19},{11,18},{12,21},{13,20},{14,23},{15,22},{24,... | collective-permute-start | bytes 393224 | tf_op jit(solution)/shard_map/ppermute | solution.py:248
  8.8 15.9 %collective-permute-start = (bf16[32,16,128]{2,1,0:T(8,128)(2,1)}, bf16[32,16,128]{2,1,0:T(8,128)(2,1)}, u32[]{:S(2)}, u32[]{:S(2)}) collective-permute-start(bf16[32,16,128]{2,1,0:T(8,128)(2,1)} %get-tuple-element.24), channel_id=1, source_target_pairs={{8,16},{9,17},{10,18},{11,19},{12,20},{13,21},{14,22},{15,23},{24,... | collective-permute-start | bytes 393224 | tf_op jit(solution)/shard_map/ppermute | solution.py:248
  11.5 1.0 %copy-start.10 = (s32[16,64]{1,0:T(8,128)S(1)}, s32[16,64]{1,0:T(8,128)}, u32[]{:S(2)}) copy-start(s32[16,64]{1,0:T(8,128)} %param.19) | copy-start | bytes 12292
  11.5 1.1 %copy-start.5 = (s32[16,64]{1,0:T(8,128)S(1)}, s32[16,64]{1,0:T(8,128)}, u32[]{:S(2)}) copy-start(s32[16,64]{1,0:T(8,128)} %live.1) | copy-start | bytes 12292
  12.6 1.0 %copy-start.3 = (bf16[2,16,64,64]{3,2,1,0:T(8,128)(2,1)S(1)}, bf16[2,16,64,64]{3,2,1,0:T(8,128)(2,1)}, u32[]{:S(2)}) copy-start(bf16[2,16,64,64]{3,2,1,0:T(8,128)(2,1)} %trans.1) | copy-start | bytes 786436
  23.4 26.3 %copy-start = (bf16[8,32,16,128]{3,2,1,0:T(8,128)(2,1)}, bf16[8,32,16,128]{3,2,1,0:T(8,128)(2,1)S(1)}, u32[]{:S(2)}) copy-start(bf16[8,32,16,128]{3,2,1,0:T(8,128)(2,1)S(1)} %all-to-all-done.everyone.own) | copy-start | bytes 3145732
  24.8 20.8 %all-to-all-start.1 = ((bf16[16,144,128]{2,1,0:T(8,128)(2,1)}), bf16[16,144,128]{2,1,0:T(8,128)(2,1)S(1)}, u32[]{:S(2)}, u32[]{:S(2)}) async-start(bf16[16,144,128]{2,1,0:T(8,128)(2,1)} %shard_map.121), calls=%async_computation.1 | async-start | bytes 1179648 | tf_op jit(solution)/shard_map/all_to_all | solution.py:269
  32.6 20.8 %collective-permute-start.2 = (bf16[8,32,16,128]{3,2,1,0:T(8,128)(2,1)S(1)}, bf16[8,32,16,128]{3,2,1,0:T(8,128)(2,1)}, u32[]{:S(2)}, u32[]{:S(2)}) collective-permute-start(bf16[8,32,16,128]{3,2,1,0:T(8,128)(2,1)S(1)} %all-to-all-done.everyone.own), channel_id=1, source_target_pairs={{0,8},{8,0},{16,24},{24,16},{32,40},{40,32},{48,56},{56,48},{64,72... | collective-permute-start | bytes 3145736 | tf_op jit(solution)/shard_map/ppermute | solution.py:263
  33.9 15.8 %copy-start.2 = (bf16[2,32,16,128]{3,2,1,0:T(8,128)(2,1)}, bf16[2,32,16,128]{3,2,1,0:T(8,128)(2,1)S(1)}, u32[]{:S(2)}) copy-start(bf16[2,32,16,128]{3,2,1,0:T(8,128)(2,1)S(1)} %shard_map.123.far0) | copy-start | bytes 786436
  34.0 19.3 %collective-permute-start.5 = (bf16[2,32,16,128]{3,2,1,0:T(8,128)(2,1)S(1)}, bf16[2,32,16,128]{3,2,1,0:T(8,128)(2,1)S(1)}, u32[]{:S(2)}, u32[]{:S(2)}) collective-permute-start(bf16[2,32,16,128]{3,2,1,0:T(8,128)(2,1)S(1)} %shard_map.123.far0), channel_id=1, source_target_pairs={{0,6},{1,7},{2,0},{3,1},{4,2},{5,3},{6,4},{7,5},{8,14},{9,15},{10,... | collective-permute-start | bytes 786440 | tf_op jit(solution)/shard_map/ppermute | solution.py:267
  35.2 18.1 %collective-permute-start.4 = (bf16[2,32,16,128]{3,2,1,0:T(8,128)(2,1)S(1)}, bf16[2,32,16,128]{3,2,1,0:T(8,128)(2,1)S(1)}, u32[]{:S(2)}, u32[]{:S(2)}) collective-permute-start(bf16[2,32,16,128]{3,2,1,0:T(8,128)(2,1)S(1)} %shard_map.123.far0), channel_id=1, source_target_pairs={{0,4},{1,5},{2,6},{3,7},{4,0},{5,1},{6,2},{7,3},{8,12},{9,13},{10,... | collective-permute-start | bytes 786440 | tf_op jit(solution)/shard_map/ppermute | solution.py:267
  36.6 16.7 %collective-permute-start.3 = (bf16[2,32,16,128]{3,2,1,0:T(8,128)(2,1)S(1)}, bf16[2,32,16,128]{3,2,1,0:T(8,128)(2,1)}, u32[]{:S(2)}, u32[]{:S(2)}) collective-permute-start(bf16[2,32,16,128]{3,2,1,0:T(8,128)(2,1)S(1)} %shard_map.123.far0), channel_id=1, source_target_pairs={{0,2},{1,3},{2,4},{3,5},{4,6},{5,7},{6,0},{7,1},{8,10},{9,11},{10,... | collective-permute-start | bytes 786440 | tf_op jit(solution)/shard_map/ppermute | solution.py:267
  49.7 13.1 %all-to-all-start.2 = ((bf16[16,64,128]{2,1,0:T(8,128)(2,1)}), bf16[16,64,128]{2,1,0:T(8,128)(2,1)S(1)}, u32[]{:S(2)}, u32[]{:S(2)}) async-start(bf16[16,64,128]{2,1,0:T(8,128)(2,1)} %shard_map.122), calls=%async_computation.2 | async-start | bytes 524288 | tf_op jit(solution)/shard_map/all_to_all | solution.py:282
  53.3 0.7 copy-start.8
  53.3 0.8 copy-start.9
  62.8 1.2 %copy-start.1 = (bf16[32,128,128]{2,1,0:T(8,128)(2,1)S(1)}, bf16[32,128,128]{2,1,0:T(8,128)(2,1)}, u32[]{:S(2)}) copy-start(bf16[32,128,128]{2,1,0:T(8,128)(2,1)} %shard_map.124.near) | copy-start | bytes 3145732
  64.0 19.6 %copy-start.4 = (f32[32,16,128]{2,1,0:T(8,128)S(1)}, f32[32,16,128]{2,1,0:T(8,128)}, u32[]{:S(2)}) copy-start(f32[32,16,128]{2,1,0:T(8,128)} %get-tuple-element.30.alive) | copy-start | bytes 786436
